TPU v7x, 128 devices: a whole 4x4x4 slice. The times are simulated.
128 devices in a mesh: section: 8 (over y, core), shard: 16 (over x, z).
Axes of the slice: x: 4, y: 4, z: 4, core: 2. Of those that a mesh axis runs over, the one named last changes fastest.
Arguments:
- fresh_rows: bfloat16 [8, 16, 8, 64, 4096], P('section', 'shard'), may hold values from -0.09375 to 0.09375
- row_bounds: int32 [8, 129], replicated, may hold values from 0 to 6144, as said below
- layer_section: int32 [8], replicated, may hold values from 0 to 7, each once
- rows_in: bfloat16 [2, 16, 4096], replicated, may hold values from -6 to 6
- attn_norm: bfloat16 [8, 4096], P('section'), may hold values from 0.099609375 to 1.8984375
- q_proj: bfloat16 [8, 4096, 4096], P('section', None, 'shard'), may hold values from -0.09375 to 0.09375
- kv_proj: bfloat16 [8, 4096, 512], P('section', None, 'shard'), may hold values from -0.09375 to 0.09375
- o_proj: bfloat16 [8, 4096, 4096], P('section', 'shard'), may hold values from -0.09375 to 0.09375
- kv_cache: bfloat16 [8, 2, 16, 2, 2, 64, 128], P('section'), may hold values from -200 to 200
- cache_lengths: int32 [2, 16], replicated, may hold values from 1 to 64, 512 in all within a row
- moe_norm: bfloat16 [8, 4096], P('section'), may hold values from 0.099609375 to 1.8984375
- router: bfloat16 [8, 4096, 2], P('section'), may hold values from -13 to 13
- expert_ids: int32 [8, 2, 16], P('section'), may hold values from 0 to 1
Outputs:
- packed: bfloat16 [8, 16, 384, 4096], P('section', 'shard')
- block_scales: float32 [8, 16, 3, 32], P('section', 'shard')
- section_out: bfloat16 [8, 2, 16, 4096], P('section', None, 'shard')
Inputs may be any that keep to these rules, and one draw needn't show every extreme that they name: row_bounds[l, 0] = 0 and row_bounds[l, 128] = 6144; every row_bounds[l, o] is within 8 of 48 * o, so an owner holds 32 to 64 rows of a layer, and in every layer some owner holds exactly 64. `cache_lengths`: the 16 rows of one micro-batch hold 512 cached positions in all, and in each micro-batch some row holds 64.
All inputs are finite; a program needn't handle non-finite values.
Results may differ from a plain program's by a relative error of at most 0.035.
Values may be sent and summed in bfloat16 or wider, within the bound.
No kernel may reach another device: no remote copies, remote signals or barrier semaphores. Data moves between devices by JAX's collectives and lax.ppermute only.
A program may use at most 128 MiB of HBM per device.

v0:
```python
import jax
import jax.numpy as jnp
from jax import lax
from jax.sharding import PartitionSpec as P

HD = 128
HEADS = 32
KVH = 2
HW = 1024
EXPS = 2
QB = 128
EDGE = 8


CODE_LIMIT = 448.0
NORM_EPSILON = 1e-06


def padded(cells, sides, width):
    for axis, dim in sides:
        count = lax.axis_size(axis)
        head = lax.slice_in_dim(cells, 0, width, axis=dim)
        tail = lax.slice_in_dim(cells, cells.shape[dim] - width, cells.shape[dim], axis=dim)
        cells = jnp.concatenate(
            [
                lax.ppermute(tail, axis, [(i, (i + 1) % count) for i in range(count)]),
                cells,
                lax.ppermute(head, axis, [((i + 1) % count, i) for i in range(count)]),
            ],
            axis=dim,
        )
    return cells


def from_behind(value, axis, steps):
    count = lax.axis_size(axis)
    initial, last = (max(0, -steps), min(count, count - steps))
    return lax.ppermute(value, axis, [(source, source + steps) for source in range(initial, last)])


def rms_scale(values, gain):
    wide = values.astype(jnp.float32)
    mean_sq = jnp.mean(wide * wide, axis=-1, keepdims=True)
    return (wide * lax.rsqrt(mean_sq + NORM_EPSILON) * gain.astype(jnp.float32)).astype(
        jnp.bfloat16
    )


def block_quantize(rows):
    count_r, width = rows.shape
    tiles = rows.astype(jnp.float32).reshape(count_r // QB, QB, width // QB, QB)
    peak = jnp.max(jnp.abs(tiles), axis=(1, 3))
    scale = (peak + 1e-06) / CODE_LIMIT
    coded = (tiles / scale[:, None, :, None]).astype(jnp.bfloat16).reshape(count_r, width)
    return (coded, scale)


def place_rows(pieces, offsets, counts, width):

    def place_one(piece, offset, count):
        keep = jnp.arange(piece.shape[0], dtype=jnp.int32)[:, None] < count
        masked = jnp.where(keep, piece, jnp.zeros_like(piece))
        base = jnp.zeros((width, piece.shape[1]), piece.dtype)
        return lax.dynamic_update_slice(base, masked, (offset, jnp.int32(0)))

    return jax.vmap(place_one)(pieces, offsets, counts)


def dequant_in(normed, coded, scale):
    batch = normed.shape[0]
    units, width = coded.shape
    parts = jnp.einsum(
        "bcj,uicj->buic",
        normed.reshape(batch, width // QB, QB),
        coded.reshape(units // QB, QB, width // QB, QB),
        preferred_element_type=jnp.float32,
    )
    return jnp.sum(parts * scale[None, :, None, :], axis=3).reshape(batch, units)


def dequant_out(hidden, coded, scale):
    batch = hidden.shape[0]
    units, width = coded.shape
    parts = jnp.einsum(
        "bui,uicj->bucj",
        hidden.reshape(batch, units // QB, QB),
        coded.reshape(units // QB, QB, width // QB, QB),
        preferred_element_type=jnp.float32,
    )
    return jnp.sum(parts * scale[None, :, :, None], axis=1).reshape(batch, width)


def expert_term(normed, coded, scale, units):
    tiles_u = units // QB
    gate = dequant_in(normed, coded[:units], scale[:tiles_u])
    upper = dequant_in(normed, coded[units : 2 * units], scale[tiles_u : 2 * tiles_u])
    hidden = (jax.nn.silu(gate) * upper).astype(jnp.bfloat16)
    return dequant_out(hidden, coded[2 * units :], scale[2 * tiles_u :])


def attend(queries, keys, values, new_key, new_value, lengths):
    factor = HD ** (-0.5)
    scores = jnp.einsum("bhd,btd->bht", queries, keys, preferred_element_type=jnp.float32) * factor
    own_score = (
        jnp.einsum("bhd,bd->bh", queries, new_key, preferred_element_type=jnp.float32) * factor
    )
    live = jnp.arange(keys.shape[1], dtype=jnp.int32)[None, None, :] < lengths[:, None, None]
    scores = jnp.where(live, scores, -1e30)
    peak = jnp.maximum(jnp.max(scores, axis=2), own_score)
    weights = jnp.where(live, jnp.exp(scores - peak[..., None]), 0.0)
    own = jnp.exp(own_score - peak)
    total = jnp.sum(weights, axis=2) + own
    weights = (weights / total[..., None]).astype(jnp.bfloat16)
    own = (own / total).astype(jnp.bfloat16)
    mixed = jnp.einsum("bht,btd->bhd", weights, values, preferred_element_type=jnp.float32)
    mixed = mixed + own.astype(jnp.float32)[..., None] * new_value.astype(jnp.float32)[:, None, :]
    return mixed.astype(jnp.bfloat16)


def local(
    fresh_rows,
    row_bounds,
    layer_section,
    rows_in,
    attn_norm,
    q_proj,
    kv_proj,
    o_proj,
    kv_cache,
    cache_lengths,
    moe_norm,
    router,
    expert_ids,
):
    sections = lax.axis_size("section")
    shards = lax.axis_size("shard")
    section_pos = lax.axis_index("section")
    shard_pos = lax.axis_index("shard")
    units = HW * EXPS // shards
    rows_dev = 3 * units
    piece = rows_dev // sections
    width = piece + 4 * EDGE
    pieces = fresh_rows[0, 0]
    layer_ids = jnp.arange(layer_section.shape[0], dtype=jnp.int32)
    order = jnp.sum(
        jnp.where(layer_section[None, :] == layer_ids[:, None], layer_ids[None, :], 0), axis=1
    )
    outgoing = jnp.take(pieces, order, axis=0)
    arrived = lax.all_to_all(outgoing, "section", split_axis=0, concat_axis=0, tiled=True)
    my_layer = lax.dynamic_index_in_dim(order, section_pos, 0, keepdims=False)
    bounds = lax.dynamic_index_in_dim(row_bounds, my_layer, 0, keepdims=False)
    owners = jnp.arange(sections, dtype=jnp.int32) * shards + shard_pos
    starts = jnp.take(bounds, owners)
    ends = jnp.take(bounds, owners + 1)
    placed = place_rows(arrived, starts - (piece * owners - EDGE), ends - starts, width)
    rims = jnp.concatenate((placed[:, :EDGE], placed[:, piece + EDGE : piece + 2 * EDGE]), axis=1)
    grown = padded(rims, (("shard", 1),), EDGE)
    from_left = grown[:, :EDGE]
    from_right = grown[:, 3 * EDGE :]
    blank = jnp.zeros_like(from_left[:1])
    from_left = jnp.where(
        shard_pos == 0, jnp.concatenate((blank, from_left[:-1]), axis=0), from_left
    )
    from_right = jnp.where(
        shard_pos == shards - 1, jnp.concatenate((from_right[1:], blank), axis=0), from_right
    )
    target = placed[:, EDGE : EDGE + piece]
    target = target.at[:, :EDGE].add(from_left)
    target = target.at[:, piece - EDGE :].add(from_right)
    gathered_rows = target.reshape(rows_dev, pieces.shape[2])
    coded, scale = block_quantize(gathered_rows)
    heads_dev = q_proj.shape[2] // HD
    group = HEADS // KVH
    shared_head = shard_pos * heads_dev // group
    expert_pos = shard_pos // (shards // EXPS)
    micro = rows_in.shape[0]
    batch = rows_in.shape[1]
    share = batch // shards
    ticks = sections + micro - 1
    attention_gain = attn_norm[0]
    expert_gain = moe_norm[0]
    query_weight = q_proj[0]
    pair_weight = kv_proj[0]
    output_weight = o_proj[0]
    router_weight = router[0]
    cache_local = kv_cache[0]
    chosen_all = expert_ids[0]

    def entry(tick):
        start_rows = lax.dynamic_index_in_dim(
            rows_in, jnp.clip(tick, 0, micro - 1), 0, keepdims=False
        )
        return start_rows

    def run_layer(state, slot_pos):
        lengths = lax.dynamic_index_in_dim(cache_lengths, slot_pos, 0, keepdims=False)
        chosen = lax.dynamic_index_in_dim(chosen_all, slot_pos, 0, keepdims=False)
        cached = lax.dynamic_index_in_dim(cache_local, slot_pos, 0, keepdims=False)
        keys = lax.dynamic_index_in_dim(cached[:, 0], shared_head, 1, keepdims=False)
        values = lax.dynamic_index_in_dim(cached[:, 1], shared_head, 1, keepdims=False)
        normed = rms_scale(state, attention_gain)
        queries = jnp.dot(normed, query_weight, preferred_element_type=jnp.float32).astype(
            jnp.bfloat16
        )
        queries = queries.reshape(batch, heads_dev, HD)
        fresh_part = jnp.dot(normed, pair_weight, preferred_element_type=jnp.float32).astype(
            jnp.bfloat16
        )
        fresh_pair = lax.all_gather(fresh_part, "shard", axis=1, tiled=True)
        new_key = lax.dynamic_slice_in_dim(fresh_pair, shared_head * HD, HD, 1)
        new_value = lax.dynamic_slice_in_dim(fresh_pair, (KVH + shared_head) * HD, HD, 1)
        mixed = attend(queries, keys, values, new_key, new_value, lengths).reshape(
            batch, heads_dev * HD
        )
        attention_term = jnp.dot(mixed, output_weight, preferred_element_type=jnp.float32)
        residual = state.astype(jnp.float32) + lax.psum(attention_term, "shard")
        expert_input = rms_scale(residual, expert_gain)
        logits = jnp.dot(expert_input, router_weight, preferred_element_type=jnp.float32)
        route_probs = jax.nn.softmax(logits, axis=-1)
        picked = chosen[:, None] == jnp.arange(EXPS, dtype=jnp.int32)[None, :]
        route_weight = jnp.sum(jnp.where(picked, route_probs, 0.0), axis=1)
        mine = route_weight * (chosen == expert_pos).astype(jnp.float32)
        term = expert_term(expert_input, coded, scale, units) * mine[:, None]
        updated = (residual + lax.psum(term, "shard")).astype(jnp.bfloat16)
        kept = lax.dynamic_slice_in_dim(updated, shard_pos * share, share, 0)
        return (updated, kept)

    def tick_step(tick, carry):
        incoming, outputs = carry
        state = jnp.where(section_pos == 0, entry(tick), incoming)
        micro_pos = tick - section_pos
        active = (micro_pos >= 0) & (micro_pos < micro)
        slot_pos = jnp.clip(micro_pos, 0, micro - 1)
        updated, kept = run_layer(state, slot_pos)
        previous = lax.dynamic_index_in_dim(outputs, slot_pos, 0, keepdims=False)
        outputs = lax.dynamic_update_index_in_dim(
            outputs, jnp.where(active, kept, previous), slot_pos, 0
        )
        incoming = from_behind(updated, "section", 1)
        return (incoming, outputs)

    starting = jnp.zeros_like(entry(0))
    outputs = jnp.zeros((micro, share, rows_in.shape[2]), jnp.bfloat16)
    _, outputs = lax.fori_loop(0, ticks, tick_step, (starting, outputs))
    return (coded[None, None], scale[None, None], outputs[None])


def solution(mesh):
    return jax.shard_map(
        local,
        mesh=mesh,
        in_specs=(
            P("section", "shard", None, None, None),
            P(),
            P(),
            P(),
            P("section", None),
            P("section", None, "shard"),
            P("section", None, "shard"),
            P("section", "shard", None),
            P("section", None, None, None, None, None, None),
            P(),
            P("section", None),
            P("section", None, None),
            P("section", None, None),
        ),
        out_specs=(
            P("section", "shard", None, None),
            P("section", "shard", None, None),
            P("section", None, "shard", None),
        ),
        check_vma=False,
    )
```

profile of v0, /device:TPU:1, one launch (start us, length us, event | category | flops | bytes accessed | tf_op | source)
XLA Modules:
  0.0 2228.7 jit_solution(2995428200997872366)
XLA Ops:
  8.0 5.0 gather_fusion
  13.0 4.6 broadcast_select_fusion.1
  17.6 6.1 all-to-all-start
  27.8 44.8 %all-to-all-done = bf16[8,64,4096]{2,1,0:T(8,128)(2,1)} async-done(((bf16[8,64,4096]{2,1,0:T(8,128)(2,1)}), bf16[8,64,4096]{2,1,0:T(8,128)(2,1)}, u32[]{:S(2)}, u32[]{:S(2)}) %all-to-all-start) | async-done | bytes 4194336 | tf_op jit(solution)/shard_map/all_to_all | solution.py:149
  72.6 4.5 broadcast_select_fusion.2
  80.1 93.0 %while.21 = (s32[]{:T(128)}, bf16[8,80,4096]{2,1,0:T(8,128)(2,1)}, s32[8,3]{0,1:T(4,128)S(1)}, bf16[8,64,4096]{2,1,0:T(8,128)(2,1)}, s32[]{:T(128)}, /*index=5*/s32[3]{0:T(128)S(1)}, s32[]{:T(128)}) while((s32[]{:T(128)}, bf16[8,80,4096]{2,1,0:T(8,128)(2,1)}, s32[8,3]{0,1:T(4,128)S(1)}, bf16[8,64,4096]{2,1,0:T(8,128)(2,1)}, s32[]{:T(128)}, ...), condition=%wide.while_cond.2, body=%wide.while_body.2.sunk | while | flops 262163 | bytes 2621619 | solution.py:64
  83.4 3.4 dynamic-slice_select_fusion.2
  86.8 5.0 dynamic-update-slice.9
  98.6 4.6 dynamic-update-slice.9
  106.5 3.4 dynamic-slice_select_fusion.2
  109.9 5.1 dynamic-update-slice.9
  118.4 3.4 dynamic-slice_select_fusion.2
  121.8 5.1 dynamic-update-slice.9
  130.3 3.3 dynamic-slice_select_fusion.2
  133.6 4.6 dynamic-update-slice.9
  141.6 3.4 dynamic-slice_select_fusion.2
  145.0 5.0 dynamic-update-slice.9
  153.4 3.4 dynamic-slice_select_fusion.2
  156.7 5.0 dynamic-update-slice.9
  168.5 4.7 dynamic-update-slice.9
  178.4 4.5 collective-permute-start.2
  188.7 6.2 collective-permute-done.1
  202.9 4.2 div.130
  207.1 7.2 div.131
  214.9 8.9 fusion.45
  223.8 3.4 copy.65
  227.2 6.5 divide_convert_fusion.3
  234.4 1986.8 %while.20 = (s32[]{:T(128)}, bf16[16,4096]{1,0:T(8,128)(2,1)S(1)}, bf16[2,1,4096]{2,0,1:T(2,128)(2,1)}, pred[]{:T(512)}, bf16[2,16,4096]{2,1,0:T(8,128)(2,1)}, /...) while((s32[]{:T(128)}, bf16[16,4096]{1,0:T(8,128)(2,1)S(1)}, ...), condition=%wide.region_15.17_spmd, body=%wide.region_3.16_spmd.sunk | while | flops 125177848 | bytes 28054216 | solution.py:244
  239.3 16.1 all-gather.2
  269.8 80.8 %all-reduce.6.cloned.1.call-done = f32[16,4096]{1,0:T(8,128)} async-done(((f32[16,4096]{1,0:T(8,128)}), f32[16,4096]{1,0:T(8,128)}) %all-reduce.6.cloned.1.call-update) | async-done | bytes 262160 | tf_op jit(solution)/shard_map/while/body/eval_jaxpr/psum | solution.py:216
  360.4 83.8 %all-reduce.8.cloned.1.call-done = f32[16,4096]{1,0:T(8,128)} async-done(((f32[16,4096]{1,0:T(8,128)}), f32[16,4096]{1,0:T(8,128)}) %all-reduce.8.cloned.1.call-update) | async-done | bytes 262160 | tf_op jit(solution)/shard_map/while/body/eval_jaxpr/psum | solution.py:224
  445.9 5.0 collective-permute-start
  458.1 17.4 all-gather.2
  489.9 81.7 %all-reduce.6.cloned.1.call-done = f32[16,4096]{1,0:T(8,128)} async-done(((f32[16,4096]{1,0:T(8,128)}), f32[16,4096]{1,0:T(8,128)}) %all-reduce.6.cloned.1.call-update) | async-done | bytes 262160 | tf_op jit(solution)/shard_map/while/body/eval_jaxpr/psum | solution.py:216
  581.4 83.8 %all-reduce.8.cloned.1.call-done = f32[16,4096]{1,0:T(8,128)} async-done(((f32[16,4096]{1,0:T(8,128)}), f32[16,4096]{1,0:T(8,128)}) %all-reduce.8.cloned.1.call-update) | async-done | bytes 262160 | tf_op jit(solution)/shard_map/while/body/eval_jaxpr/psum | solution.py:224
  666.9 5.0 collective-permute-start
  679.1 17.4 all-gather.2
  710.9 81.7 %all-reduce.6.cloned.1.call-done = f32[16,4096]{1,0:T(8,128)} async-done(((f32[16,4096]{1,0:T(8,128)}), f32[16,4096]{1,0:T(8,128)}) %all-reduce.6.cloned.1.call-update) | async-done | bytes 262160 | tf_op jit(solution)/shard_map/while/body/eval_jaxpr/psum | solution.py:216
  802.4 83.8 %all-reduce.8.cloned.1.call-done = f32[16,4096]{1,0:T(8,128)} async-done(((f32[16,4096]{1,0:T(8,128)}), f32[16,4096]{1,0:T(8,128)}) %all-reduce.8.cloned.1.call-update) | async-done | bytes 262160 | tf_op jit(solution)/shard_map/while/body/eval_jaxpr/psum | solution.py:224
  887.9 5.0 collective-permute-start
  900.1 17.4 all-gather.2
  932.0 81.7 %all-reduce.6.cloned.1.call-done = f32[16,4096]{1,0:T(8,128)} async-done(((f32[16,4096]{1,0:T(8,128)}), f32[16,4096]{1,0:T(8,128)}) %all-reduce.6.cloned.1.call-update) | async-done | bytes 262160 | tf_op jit(solution)/shard_map/while/body/eval_jaxpr/psum | solution.py:216
  1023.4 83.8 %all-reduce.8.cloned.1.call-done = f32[16,4096]{1,0:T(8,128)} async-done(((f32[16,4096]{1,0:T(8,128)}), f32[16,4096]{1,0:T(8,128)}) %all-reduce.8.cloned.1.call-update) | async-done | bytes 262160 | tf_op jit(solution)/shard_map/while/body/eval_jaxpr/psum | solution.py:224
  1108.9 5.0 collective-permute-start
  1121.2 17.4 all-gather.2
  1153.0 81.7 %all-reduce.6.cloned.1.call-done = f32[16,4096]{1,0:T(8,128)} async-done(((f32[16,4096]{1,0:T(8,128)}), f32[16,4096]{1,0:T(8,128)}) %all-reduce.6.cloned.1.call-update) | async-done | bytes 262160 | tf_op jit(solution)/shard_map/while/body/eval_jaxpr/psum | solution.py:216
  1244.4 83.8 %all-reduce.8.cloned.1.call-done = f32[16,4096]{1,0:T(8,128)} async-done(((f32[16,4096]{1,0:T(8,128)}), f32[16,4096]{1,0:T(8,128)}) %all-reduce.8.cloned.1.call-update) | async-done | bytes 262160 | tf_op jit(solution)/shard_map/while/body/eval_jaxpr/psum | solution.py:224
  1329.9 5.0 collective-permute-start
  1342.2 17.4 all-gather.2
  1374.0 81.7 %all-reduce.6.cloned.1.call-done = f32[16,4096]{1,0:T(8,128)} async-done(((f32[16,4096]{1,0:T(8,128)}), f32[16,4096]{1,0:T(8,128)}) %all-reduce.6.cloned.1.call-update) | async-done | bytes 262160 | tf_op jit(solution)/shard_map/while/body/eval_jaxpr/psum | solution.py:216
  1465.4 83.8 %all-reduce.8.cloned.1.call-done = f32[16,4096]{1,0:T(8,128)} async-done(((f32[16,4096]{1,0:T(8,128)}), f32[16,4096]{1,0:T(8,128)}) %all-reduce.8.cloned.1.call-update) | async-done | bytes 262160 | tf_op jit(solution)/shard_map/while/body/eval_jaxpr/psum | solution.py:224
  1550.9 5.0 collective-permute-start
  1563.2 17.4 all-gather.2
  1595.0 81.7 %all-reduce.6.cloned.1.call-done = f32[16,4096]{1,0:T(8,128)} async-done(((f32[16,4096]{1,0:T(8,128)}), f32[16,4096]{1,0:T(8,128)}) %all-reduce.6.cloned.1.call-update) | async-done | bytes 262160 | tf_op jit(solution)/shard_map/while/body/eval_jaxpr/psum | solution.py:216
  1686.4 83.8 %all-reduce.8.cloned.1.call-done = f32[16,4096]{1,0:T(8,128)} async-done(((f32[16,4096]{1,0:T(8,128)}), f32[16,4096]{1,0:T(8,128)}) %all-reduce.8.cloned.1.call-update) | async-done | bytes 262160 | tf_op jit(solution)/shard_map/while/body/eval_jaxpr/psum | solution.py:224
  1771.9 5.0 collective-permute-start
  1784.2 17.4 all-gather.2
  1816.0 81.7 %all-reduce.6.cloned.1.call-done = f32[16,4096]{1,0:T(8,128)} async-done(((f32[16,4096]{1,0:T(8,128)}), f32[16,4096]{1,0:T(8,128)}) %all-reduce.6.cloned.1.call-update) | async-done | bytes 262160 | tf_op jit(solution)/shard_map/while/body/eval_jaxpr/psum | solution.py:216
  1907.4 83.8 %all-reduce.8.cloned.1.call-done = f32[16,4096]{1,0:T(8,128)} async-done(((f32[16,4096]{1,0:T(8,128)}), f32[16,4096]{1,0:T(8,128)}) %all-reduce.8.cloned.1.call-update) | async-done | bytes 262160 | tf_op jit(solution)/shard_map/while/body/eval_jaxpr/psum | solution.py:224
  1992.9 5.0 collective-permute-start
  2005.2 17.4 all-gather.2
  2037.0 81.7 %all-reduce.6.cloned.1.call-done = f32[16,4096]{1,0:T(8,128)} async-done(((f32[16,4096]{1,0:T(8,128)}), f32[16,4096]{1,0:T(8,128)}) %all-reduce.6.cloned.1.call-update) | async-done | bytes 262160 | tf_op jit(solution)/shard_map/while/body/eval_jaxpr/psum | solution.py:216
  2128.4 83.8 %all-reduce.8.cloned.1.call-done = f32[16,4096]{1,0:T(8,128)} async-done(((f32[16,4096]{1,0:T(8,128)}), f32[16,4096]{1,0:T(8,128)}) %all-reduce.8.cloned.1.call-update) | async-done | bytes 262160 | tf_op jit(solution)/shard_map/while/body/eval_jaxpr/psum | solution.py:224
  2213.9 5.0 collective-permute-start
  (512 shorter events, 357.4 us)
Async XLA Ops:
  7.2 19.1 copy-start
  17.6 10.0 copy-start.10
  17.6 55.0 %all-to-all-start = ((bf16[8,64,4096]{2,1,0:T(8,128)(2,1)}), bf16[8,64,4096]{2,1,0:T(8,128)(2,1)}, u32[]{:S(2)}, u32[]{:S(2)}) async-start(bf16[8,64,4096]{2,1,0:T(8,128)(2,1)} %broadcast_select_fusion.1), calls=%async_computation | async-start | bytes 8388608 | tf_op jit(solution)/shard_map/all_to_all | solution.py:149
  77.1 3.0 copy-start.8
  80.1 102.8 %copy-start.4 = (bf16[1,2,16,2,2,64,128]{6,5,4,3,2,1,0:T(8,128)(2,1)S(1)}, bf16[1,2,16,2,2,64,128]{6,5,4,3,2,1,0:T(8,128)(2,1)}, u32[]{:S(2)}) copy-start(bf16[1,2,16,2,2,64,128]{6,5,4,3,2,1,0:T(8,128)(2,1)} %param.29) | copy-start | bytes 6291460
  173.1 11.4 copy-start.5
  173.1 12.7 copy-start.6
  173.1 12.8 copy-start.7
  175.4 19.4 collective-permute-start.1
  178.4 17.5 collective-permute-start.2
  199.7 15.2 copy-start.3
  234.4 116.3 %all-reduce.6.cloned.1.call-start = ((), (), s32[]{:S(2)}) async-start(), calls=%async_computation.1 | async-start | bytes 524288 | tf_op jit(solution)/shard_map/while/body/eval_jaxpr/psum | solution.py:216
  263.9 180.2 %all-reduce.8.cloned.1.call-start = ((), (), s32[]{:S(2)}) async-start(), calls=%async_computation.2 | async-start | bytes 524288 | tf_op jit(solution)/shard_map/while/body/eval_jaxpr/psum | solution.py:224
  350.6 8.1 copy-start.9
  350.6 93.5 %copy-start.2 = (f32[16,4096]{1,0:T(8,128)S(1)}, f32[16,4096]{1,0:T(8,128)}, u32[]{:S(2)}) copy-start(f32[16,4096]{1,0:T(8,128)} %all-reduce.6.cloned.1.call-done) | copy-start | bytes 786436 | tf_op jit(solution)/shard_map/while
  445.9 7.3 collective-permute-start
  453.2 118.5 %all-reduce.6.cloned.1.call-start = ((), (), s32[]{:S(2)}) async-start(), calls=%async_computation.1 | async-start | bytes 524288 | tf_op jit(solution)/shard_map/while/body/eval_jaxpr/psum | solution.py:216
  484.0 181.1 %all-reduce.8.cloned.1.call-start = ((), (), s32[]{:S(2)}) async-start(), calls=%async_computation.2 | async-start | bytes 524288 | tf_op jit(solution)/shard_map/while/body/eval_jaxpr/psum | solution.py:224
  571.7 8.1 copy-start.9
  571.7 93.5 %copy-start.2 = (f32[16,4096]{1,0:T(8,128)S(1)}, f32[16,4096]{1,0:T(8,128)}, u32[]{:S(2)}) copy-start(f32[16,4096]{1,0:T(8,128)} %all-reduce.6.cloned.1.call-done) | copy-start | bytes 786436 | tf_op jit(solution)/shard_map/while
  666.9 7.3 collective-permute-start
  674.2 118.5 %all-reduce.6.cloned.1.call-start = ((), (), s32[]{:S(2)}) async-start(), calls=%async_computation.1 | async-start | bytes 524288 | tf_op jit(solution)/shard_map/while/body/eval_jaxpr/psum | solution.py:216
  705.1 181.1 %all-reduce.8.cloned.1.call-start = ((), (), s32[]{:S(2)}) async-start(), calls=%async_computation.2 | async-start | bytes 524288 | tf_op jit(solution)/shard_map/while/body/eval_jaxpr/psum | solution.py:224
  792.7 8.1 copy-start.9
  792.7 93.5 %copy-start.2 = (f32[16,4096]{1,0:T(8,128)S(1)}, f32[16,4096]{1,0:T(8,128)}, u32[]{:S(2)}) copy-start(f32[16,4096]{1,0:T(8,128)} %all-reduce.6.cloned.1.call-done) | copy-start | bytes 786436 | tf_op jit(solution)/shard_map/while
  887.9 7.3 collective-permute-start
  895.2 118.5 %all-reduce.6.cloned.1.call-start = ((), (), s32[]{:S(2)}) async-start(), calls=%async_computation.1 | async-start | bytes 524288 | tf_op jit(solution)/shard_map/while/body/eval_jaxpr/psum | solution.py:216
  926.1 181.1 %all-reduce.8.cloned.1.call-start = ((), (), s32[]{:S(2)}) async-start(), calls=%async_computation.2 | async-start | bytes 524288 | tf_op jit(solution)/shard_map/while/body/eval_jaxpr/psum | solution.py:224
  1013.7 8.1 copy-start.9
  1013.7 93.5 %copy-start.2 = (f32[16,4096]{1,0:T(8,128)S(1)}, f32[16,4096]{1,0:T(8,128)}, u32[]{:S(2)}) copy-start(f32[16,4096]{1,0:T(8,128)} %all-reduce.6.cloned.1.call-done) | copy-start | bytes 786436 | tf_op jit(solution)/shard_map/while
  1108.9 7.3 collective-permute-start
  1116.2 118.5 %all-reduce.6.cloned.1.call-start = ((), (), s32[]{:S(2)}) async-start(), calls=%async_computation.1 | async-start | bytes 524288 | tf_op jit(solution)/shard_map/while/body/eval_jaxpr/psum | solution.py:216
  1147.1 181.1 %all-reduce.8.cloned.1.call-start = ((), (), s32[]{:S(2)}) async-start(), calls=%async_computation.2 | async-start | bytes 524288 | tf_op jit(solution)/shard_map/while/body/eval_jaxpr/psum | solution.py:224
  1234.7 8.1 copy-start.9
  1234.7 93.5 %copy-start.2 = (f32[16,4096]{1,0:T(8,128)S(1)}, f32[16,4096]{1,0:T(8,128)}, u32[]{:S(2)}) copy-start(f32[16,4096]{1,0:T(8,128)} %all-reduce.6.cloned.1.call-done) | copy-start | bytes 786436 | tf_op jit(solution)/shard_map/while
  1329.9 7.3 collective-permute-start
  1337.2 118.5 %all-reduce.6.cloned.1.call-start = ((), (), s32[]{:S(2)}) async-start(), calls=%async_computation.1 | async-start | bytes 524288 | tf_op jit(solution)/shard_map/while/body/eval_jaxpr/psum | solution.py:216
  1368.1 181.1 %all-reduce.8.cloned.1.call-start = ((), (), s32[]{:S(2)}) async-start(), calls=%async_computation.2 | async-start | bytes 524288 | tf_op jit(solution)/shard_map/while/body/eval_jaxpr/psum | solution.py:224
  1455.7 8.1 copy-start.9
  1455.7 93.5 %copy-start.2 = (f32[16,4096]{1,0:T(8,128)S(1)}, f32[16,4096]{1,0:T(8,128)}, u32[]{:S(2)}) copy-start(f32[16,4096]{1,0:T(8,128)} %all-reduce.6.cloned.1.call-done) | copy-start | bytes 786436 | tf_op jit(solution)/shard_map/while
  1550.9 7.3 collective-permute-start
  1558.2 118.5 %all-reduce.6.cloned.1.call-start = ((), (), s32[]{:S(2)}) async-start(), calls=%async_computation.1 | async-start | bytes 524288 | tf_op jit(solution)/shard_map/while/body/eval_jaxpr/psum | solution.py:216
  1589.1 181.1 %all-reduce.8.cloned.1.call-start = ((), (), s32[]{:S(2)}) async-start(), calls=%async_computation.2 | async-start | bytes 524288 | tf_op jit(solution)/shard_map/while/body/eval_jaxpr/psum | solution.py:224
  1676.7 8.1 copy-start.9
  1676.7 93.5 %copy-start.2 = (f32[16,4096]{1,0:T(8,128)S(1)}, f32[16,4096]{1,0:T(8,128)}, u32[]{:S(2)}) copy-start(f32[16,4096]{1,0:T(8,128)} %all-reduce.6.cloned.1.call-done) | copy-start | bytes 786436 | tf_op jit(solution)/shard_map/while
  1771.9 7.3 collective-permute-start
  1779.2 118.5 %all-reduce.6.cloned.1.call-start = ((), (), s32[]{:S(2)}) async-start(), calls=%async_computation.1 | async-start | bytes 524288 | tf_op jit(solution)/shard_map/while/body/eval_jaxpr/psum | solution.py:216
  1810.1 181.1 %all-reduce.8.cloned.1.call-start = ((), (), s32[]{:S(2)}) async-start(), calls=%async_computation.2 | async-start | bytes 524288 | tf_op jit(solution)/shard_map/while/body/eval_jaxpr/psum | solution.py:224
  1897.7 8.1 copy-start.9
  1897.7 93.5 %copy-start.2 = (f32[16,4096]{1,0:T(8,128)S(1)}, f32[16,4096]{1,0:T(8,128)}, u32[]{:S(2)}) copy-start(f32[16,4096]{1,0:T(8,128)} %all-reduce.6.cloned.1.call-done) | copy-start | bytes 786436 | tf_op jit(solution)/shard_map/while
  1992.9 7.3 collective-permute-start
  2000.2 118.5 %all-reduce.6.cloned.1.call-start = ((), (), s32[]{:S(2)}) async-start(), calls=%async_computation.1 | async-start | bytes 524288 | tf_op jit(solution)/shard_map/while/body/eval_jaxpr/psum | solution.py:216
  2031.1 181.1 %all-reduce.8.cloned.1.call-start = ((), (), s32[]{:S(2)}) async-start(), calls=%async_computation.2 | async-start | bytes 524288 | tf_op jit(solution)/shard_map/while/body/eval_jaxpr/psum | solution.py:224
  2118.7 8.1 copy-start.9
  2118.7 93.5 %copy-start.2 = (f32[16,4096]{1,0:T(8,128)S(1)}, f32[16,4096]{1,0:T(8,128)}, u32[]{:S(2)}) copy-start(f32[16,4096]{1,0:T(8,128)} %all-reduce.6.cloned.1.call-done) | copy-start | bytes 786436 | tf_op jit(solution)/shard_map/while
  2213.9 7.3 collective-permute-start
  2221.2 0.7 copy-start.1
Sparse Core Ops, SparseCore 0:
  264.1 86.5 all-reduce.5
  360.5 83.6 all-reduce.7
  484.2 87.4 all-reduce.5
  581.5 83.6 all-reduce.7
  705.2 87.4 all-reduce.5
  802.5 83.6 all-reduce.7
  926.2 87.4 all-reduce.5
  1023.5 83.6 all-reduce.7
  1147.2 87.4 all-reduce.5
  1244.5 83.6 all-reduce.7
  1368.2 87.4 all-reduce.5
  1465.5 83.6 all-reduce.7
  1589.2 87.4 all-reduce.5
  1686.5 83.6 all-reduce.7
  1810.2 87.4 all-reduce.5
  1907.5 83.6 all-reduce.7
  2031.2 87.4 all-reduce.5
  2128.5 83.6 all-reduce.7
where the time goes:
time: 2240 us; the launch traced here: 2230 us
  waiting for transfers between devices  1540 us (69%)
  local copies, waits for them, and re-layouts  165 us (7%)
  other arithmetic  161 us (7%)
  blocking collectives  155 us (7%)
  matrix products  131 us (6%)
  starting transfers between devices  58.6 us (3%)
    psum x9, waiting for transfers between devices, run_layer(): updated = (residual + lax.psum(term, 'shard')).astype(jnp.bfloat16)  754 us
    psum x9, waiting for transfers between devices, run_layer(): residual = state.astype(jnp.float32) + lax.psum(attention_term, 'shard')  734 us
    all_gather x9, blocking collectives, run_layer(): fresh_pair = lax.all_gather(fresh_part, 'shard', axis=1, tiled=True)  155 us
    scatter x16, other arithmetic  48.5 us
    all_to_all x1, waiting for transfers between devices, local(): lax.all_to_all(outgoing, 'section', split_axis=0, concat_axis=0, tiled=True)  44.8 us
  transfers between devices with their start and end apart: 30, of which 20 were waited for; matrix products, arithmetic and copies ran while one was open for 4% of the time, Pallas kernels for 0%

commit v1 on v0

v1 whole, which is shorter than its diff:
```python
import jax
import jax.numpy as jnp
from jax import lax
from jax.experimental import pallas as pl
from jax.experimental.pallas import tpu as pltpu
from jax.sharding import PartitionSpec as P

HD = 128
HEADS = 32
KVH = 2
EXPS = 2
QB = 128
EDGE = 8
PIECE = 48
CODE_LIMIT = 448.0
NORM_EPSILON = 1e-06
MIB = 1024 * 1024

bf16 = jnp.bfloat16
f32 = jnp.float32
NT = (((1,), (1,)), ((), ()))


def pairs_of(move):
    result = []
    for s in range(8):
        for x in range(4):
            for z in range(4):
                s2, x2, z2 = move(s, x, z)
                result.append((s * 16 + x * 4 + z, s2 % 8 * 16 + x2 % 4 * 4 + z2 % 4))
    return result


AXES = ("section", "shard")


def send(value, move):
    return lax.ppermute(value, AXES, pairs_of(move))


def share_kernel(order, starts, ends, base, piece_ref, left_ref, right_ref, out_ref):
    d = pl.program_id(0)
    layer = order[d]
    first = starts[layer] - base[0]
    stop = ends[layer] - base[0]
    t = lax.broadcasted_iota(jnp.int32, (PIECE, 64), 0)
    r = lax.broadcasted_iota(jnp.int32, (PIECE, 64), 1)
    own = jnp.where((r == t - first) & (t < stop), 1.0, 0.0).astype(bf16)
    t = lax.broadcasted_iota(jnp.int32, (PIECE, 16), 0)
    r = lax.broadcasted_iota(jnp.int32, (PIECE, 16), 1)
    near = (r < 8) & (r == t) & (t < first)
    far = (r >= 8) & (r - 8 == t - stop) & (t >= stop)
    rim = jnp.where(near | far, 1.0, 0.0).astype(bf16)
    rims = jnp.concatenate((left_ref[0].astype(f32), right_ref[0].astype(f32)), axis=0).astype(bf16)
    total = jnp.dot(own, piece_ref[0], preferred_element_type=f32)
    total = total + jnp.dot(rim, rims, preferred_element_type=f32)
    out_ref[0] = total.astype(bf16)


def build_shares(order, starts, ends, base, pieces, from_left, from_right):
    layers, slots, width = pieces.shape
    return pl.pallas_call(
        share_kernel,
        grid_spec=pltpu.PrefetchScalarGridSpec(
            num_scalar_prefetch=4,
            grid=(layers,),
            in_specs=[
                pl.BlockSpec((1, slots, width), lambda d, o, *_: (o[d], 0, 0)),
                pl.BlockSpec((1, EDGE, width), lambda d, o, *_: (o[d], 0, 0)),
                pl.BlockSpec((1, EDGE, width), lambda d, o, *_: (o[d], 0, 0)),
            ],
            out_specs=pl.BlockSpec((1, PIECE, width), lambda d, *_: (d, 0, 0)),
        ),
        out_shape=jax.ShapeDtypeStruct((layers, PIECE, width), bf16),
        compiler_params=pltpu.CompilerParams(vmem_limit_bytes=24 * MIB),
        name="build_shares",
    )(order, starts, ends, base, pieces, from_left, from_right)


def quantize_kernel(rows_ref, coded_ref, scale_ref):
    step = pl.program_id(0)
    rows, width = rows_ref.shape
    cols = width // QB
    at_r = lax.broadcasted_iota(jnp.int32, scale_ref.shape, 0)
    at_c = lax.broadcasted_iota(jnp.int32, scale_ref.shape, 1)
    scales = jnp.where(step == 0, jnp.zeros(scale_ref.shape, f32), scale_ref[...])
    for i in range(rows // QB):
        for c in range(cols):
            tile = rows_ref[i * QB : (i + 1) * QB, c * QB : (c + 1) * QB].astype(f32)
            peak = jnp.max(jnp.max(jnp.abs(tile), axis=0, keepdims=True), axis=1, keepdims=True)
            scale = (peak + 1e-06) / CODE_LIMIT
            coded_ref[i * QB : (i + 1) * QB, c * QB : (c + 1) * QB] = (tile * (1.0 / scale)).astype(bf16)
            scales = jnp.where((at_r == i) & (at_c == step * cols + c), scale, scales)
    scale_ref[...] = scales


def quantize(rows):
    count, width = rows.shape
    chunk = 1024
    return pl.pallas_call(
        quantize_kernel,
        grid=(width // chunk,),
        in_specs=[pl.BlockSpec((count, chunk), lambda i: (0, i))],
        out_specs=[
            pl.BlockSpec((count, chunk), lambda i: (0, i)),
            pl.BlockSpec((count // QB, width // QB), lambda i: (0, 0)),
        ],
        out_shape=[
            jax.ShapeDtypeStruct((count, width), bf16),
            jax.ShapeDtypeStruct((count // QB, width // QB), f32),
        ],
        compiler_params=pltpu.CompilerParams(vmem_limit_bytes=24 * MIB),
        name="quantize",
    )(rows)


def rms(wide, gain):
    mean_sq = jnp.mean(wide * wide, axis=-1, keepdims=True)
    return (wide * lax.rsqrt(mean_sq + NORM_EPSILON) * gain.astype(f32)).astype(bf16)


def attention_kernel(tick, flags, place, *refs):
    (parts, gain, bounds, wq, wkv, wo, cache) = (refs[:4],) + refs[4:10]
    state, out, keep = refs[10:13]
    vq, vkv, vo, vk, vv, sems = refs[13:]

    @pl.when(flags[tick] == 1)
    def _():
        head = place[0]
        row = place[1]
        copies = [
            pltpu.make_async_copy(wq, vq, sems.at[0]),
            pltpu.make_async_copy(wkv.at[pl.ds(head * 4, 4)], vkv.at[pl.ds(0, 4)], sems.at[1]),
            pltpu.make_async_copy(wkv.at[pl.ds(8 + head * 4, 4)], vkv.at[pl.ds(4, 4)], sems.at[2]),
            pltpu.make_async_copy(cache.at[:, :, 0, head], vk, sems.at[3]),
            pltpu.make_async_copy(cache.at[:, :, 1, head], vv, sems.at[4]),
            pltpu.make_async_copy(wo, vo, sems.at[5]),
        ]
        for copy in copies:
            copy.start()
        total = parts[0][...].astype(f32)
        for part in parts[1:]:
            total = total + part[...].astype(f32)
        rounded = total.astype(bf16)
        state[...] = rounded
        rows = rounded.shape[0]
        wide = rounded.astype(f32)
        pick = lax.broadcasted_iota(jnp.int32, (rows, 1), 0)
        for micro in range(2):
            chosen = jnp.where(pick == micro * 16 + row, wide, 0.0)
            keep[micro : micro + 1, :] = jnp.sum(chosen, axis=0, keepdims=True)
        normed = rms(wide, gain[...])
        copies[0].wait()
        q = jnp.dot(normed, vq[...], preferred_element_type=f32).astype(bf16)
        copies[1].wait()
        copies[2].wait()
        pair = lax.dot_general(normed, vkv[...].reshape(2 * HD, -1), NT, preferred_element_type=f32)
        pair = pair.astype(bf16)
        q2 = jnp.concatenate((q[:, :HD], q[:, HD:]), axis=0)
        new_key = jnp.concatenate((pair[:, :HD], pair[:, :HD]), axis=0)
        new_value = jnp.concatenate((pair[:, HD:], pair[:, HD:]), axis=0).astype(f32)
        factor = HD ** (-0.5)
        own_score = jnp.sum(q2.astype(f32) * new_key.astype(f32), axis=-1, keepdims=True) * factor
        copies[3].wait()
        scores = lax.dot_general(q2, vk[...].reshape(-1, HD), NT, preferred_element_type=f32) * factor
        at = lax.broadcasted_iota(jnp.int32, scores.shape, 1)
        live = (at >= bounds[:, 0:1]) & (at < bounds[:, 1:2])
        scores = jnp.where(live, scores, -1e30)
        peak = jnp.maximum(jnp.max(scores, axis=-1, keepdims=True), own_score)
        weights = jnp.where(live, jnp.exp(scores - peak), 0.0)
        own = jnp.exp(own_score - peak)
        whole = jnp.sum(weights, axis=-1, keepdims=True) + own
        weights = (weights / whole).astype(bf16)
        own = (own / whole).astype(bf16).astype(f32)
        copies[4].wait()
        mixed = jnp.dot(weights, vv[...].reshape(-1, HD), preferred_element_type=f32)
        mixed = (mixed + own * new_value).astype(bf16)
        mixed = jnp.concatenate((mixed[:rows], mixed[rows:]), axis=1)
        copies[5].wait()
        out[...] = jnp.dot(mixed, vo[...], preferred_element_type=f32).astype(bf16)


def any_spec():
    return pl.BlockSpec(memory_space=pl.ANY)


def smem_spec():
    return pl.BlockSpec(memory_space=pltpu.SMEM)


def vmem_spec():
    return pl.BlockSpec(memory_space=pltpu.VMEM)


def attention(tick, flags, place, parts, gain, bounds, wq, wkv, wo, cache):
    rows, width = parts[0].shape
    mine = wq.shape[1]
    micro, batch, _, _, ctx, hd = cache.shape
    return pl.pallas_call(
        lambda *refs: attention_kernel(tick, *refs),
        in_specs=[smem_spec(), smem_spec()]
        + [vmem_spec()] * 6
        + [any_spec()] * 4,
        out_specs=[vmem_spec(), vmem_spec(), vmem_spec()],
        out_shape=[
            jax.ShapeDtypeStruct((rows, width), bf16),
            jax.ShapeDtypeStruct((rows, width), bf16),
            jax.ShapeDtypeStruct((2, width), f32),
        ],
        scratch_shapes=[
            pltpu.VMEM(wq.shape, bf16),
            pltpu.VMEM((8, 2 * HD // 8, width), bf16),
            pltpu.VMEM(wo.shape, bf16),
            pltpu.VMEM((micro, batch, ctx, hd), bf16),
            pltpu.VMEM((micro, batch, ctx, hd), bf16),
            pltpu.SemaphoreType.DMA((6,)),
        ],
        compiler_params=pltpu.CompilerParams(vmem_limit_bytes=28 * MIB),
        name="attention",
    )(flags, place, *parts, gain, bounds, wq, wkv, wo, cache)


def expert_kernel(tick, flags, place, *refs):
    state, parts, gain, router, chosen, rows_ref, out, vw, sems = (
        refs[0],
        refs[1:5],
    ) + refs[5:]

    @pl.when(flags[tick] == 1)
    def _():
        units = vw.shape[0] // 3
        copies = [
            pltpu.make_async_copy(rows_ref.at[pl.ds(0, 2 * units)], vw.at[pl.ds(0, 2 * units)], sems.at[0]),
            pltpu.make_async_copy(rows_ref.at[pl.ds(2 * units, units)], vw.at[pl.ds(2 * units, units)], sems.at[1]),
        ]
        for copy in copies:
            copy.start()
        total = parts[0][...].astype(f32)
        for part in parts[1:]:
            total = total + part[...].astype(f32)
        residual = state[...].astype(f32) + total
        entry = rms(residual, gain[...])
        wide = entry.astype(f32)
        first = jnp.sum(wide * router[0:1, :].astype(f32), axis=-1, keepdims=True)
        second = jnp.sum(wide * router[1:2, :].astype(f32), axis=-1, keepdims=True)
        peak = jnp.maximum(first, second)
        first = jnp.exp(first - peak)
        second = jnp.exp(second - peak)
        expert = place[2]
        prob = jnp.where(expert == 0, first, second) / (first + second)
        mine = jnp.where(chosen[...] == expert, prob, 0.0)
        copies[0].wait()
        both = lax.dot_general(entry, vw[0 : 2 * units, :], NT, preferred_element_type=f32)
        gate = both[:, :units]
        hidden = (gate * jax.nn.sigmoid(gate) * both[:, units:]).astype(bf16)
        copies[1].wait()
        down = jnp.dot(hidden, vw[2 * units :, :], preferred_element_type=f32)
        once = jnp.where(place[3] == 0, 1.0, 0.0)
        out[...] = (down * mine + residual * once).astype(bf16)


def experts(tick, flags, place, state, parts, gain, router, chosen, rows):
    return pl.pallas_call(
        lambda *refs: expert_kernel(tick, *refs),
        in_specs=[smem_spec(), smem_spec()] + [vmem_spec()] * 8 + [any_spec()],
        out_specs=vmem_spec(),
        out_shape=jax.ShapeDtypeStruct(state.shape, bf16),
        scratch_shapes=[pltpu.VMEM(rows.shape, bf16), pltpu.SemaphoreType.DMA((2,))],
        compiler_params=pltpu.CompilerParams(vmem_limit_bytes=28 * MIB),
        name="experts",
    )(flags, place, state, *parts, gain, router, chosen, rows)


def sum_parts(parts):
    total = parts[0].astype(f32)
    for part in parts[1:]:
        total = total + part.astype(f32)
    return total


def local(
    fresh_rows,
    row_bounds,
    layer_section,
    rows_in,
    attn_norm,
    q_proj,
    kv_proj,
    o_proj,
    kv_cache,
    cache_lengths,
    moe_norm,
    router,
    expert_ids,
):
    sections = lax.axis_size("section")
    shards = lax.axis_size("shard")
    section_pos = lax.axis_index("section")
    shard_pos = lax.axis_index("shard")
    width = rows_in.shape[2]

    pieces = fresh_rows[0, 0]
    layer_ids = jnp.arange(layer_section.shape[0], dtype=jnp.int32)
    order = jnp.sum(
        jnp.where(layer_section[None, :] == layer_ids[:, None], layer_ids[None, :], 0), axis=1
    ).astype(jnp.int32)
    owner = section_pos * shards + shard_pos
    base = (PIECE * owner).astype(jnp.int32)
    starts = lax.dynamic_slice_in_dim(row_bounds, owner, 1, 1)[:, 0]
    ends = lax.dynamic_slice_in_dim(row_bounds, owner + 1, 1, 1)[:, 0]
    slot = jnp.arange(pieces.shape[1], dtype=jnp.int32)[None, None, :]
    edge = jnp.arange(EDGE, dtype=jnp.int32)[None, :, None]
    pick = (slot == edge + (base + PIECE - starts)[:, None, None]).astype(bf16)
    to_right = jnp.einsum("lts,lsd->ltd", pick, pieces, preferred_element_type=f32).astype(bf16)
    to_left = pieces[:, :EDGE]
    count = sections * shards
    from_left = lax.ppermute(to_right, AXES, [(i, (i + 1) % count) for i in range(count)])
    from_right = lax.ppermute(to_left, AXES, [((i + 1) % count, i) for i in range(count)])
    shares = build_shares(order, starts, ends, base[None], pieces, from_left, from_right)
    arrived = lax.all_to_all(shares, "section", split_axis=0, concat_axis=0, tiled=True)
    dest_rows = arrived.reshape(sections * PIECE, width)
    coded, scale = quantize(dest_rows)

    micro, batch, _ = rows_in.shape
    rows = micro * batch
    flags = (layer_ids == section_pos).astype(jnp.int32)
    heads_dev = q_proj.shape[2] // HD
    shared_head = shard_pos * heads_dev // (HEADS // KVH)
    expert_pos = shard_pos // (shards // EXPS)
    place = jnp.stack([shared_head, shard_pos, expert_pos, shard_pos]).astype(jnp.int32)
    pair_weight = lax.all_gather(kv_proj[0].T, "shard", axis=0)
    low = jnp.arange(rows, dtype=jnp.int32) * kv_cache.shape[5]
    high = low + cache_lengths.reshape(rows)
    bounds = jnp.tile(jnp.stack((low, high), axis=1), (heads_dev, 1))
    router_rows = router[0].T
    chosen = expert_ids[0].reshape(rows, 1)

    entry = rows_in.reshape(rows, width)
    parts = (entry, jnp.zeros_like(entry), jnp.zeros_like(entry), jnp.zeros_like(entry))
    keep = jnp.zeros((micro, width), f32)
    for tick in range(sections):
        state, term, keep_new = attention(
            tick, flags, place, parts, attn_norm, bounds, q_proj[0], pair_weight, o_proj[0], kv_cache[0]
        )
        keep = jnp.where(flags[tick] == 1, keep_new, keep)
        summed = sum_parts(
            [term] + [send(term, lambda s, x, z, k=k: (s, x, z + k)) for k in (2, 1, 3)]
        ).astype(bf16)
        around = [summed] + [send(summed, lambda s, x, z, k=k: (s, x + k, z)) for k in (2, 1, 3)]
        term = experts(tick, flags, place, state, around, moe_norm, router_rows, chosen, dest_rows)
        summed = sum_parts(
            [term] + [send(term, lambda s, x, z, k=k: (s, x, z + k)) for k in (2, 1, 3)]
        ).astype(bf16)
        parts = [send(summed, lambda s, x, z, k=k: (s + 1, x + k, z)) for k in (2, 0, 1, 3)]
    final = sum_parts(parts)
    final = jnp.stack([lax.dynamic_index_in_dim(final, m * batch + shard_pos, 0, keepdims=False) for m in range(micro)])
    keep = jnp.where(section_pos == 0, final, keep).astype(bf16)
    outputs = send(keep, lambda s, x, z: (s - 1, x, z))
    return (coded[None, None], scale[None, None], outputs[None, :, None])


def solution(mesh):
    return jax.shard_map(
        local,
        mesh=mesh,
        in_specs=(
            P("section", "shard", None, None, None),
            P(),
            P(),
            P(),
            P("section", None),
            P("section", None, "shard"),
            P("section", None, "shard"),
            P("section", "shard", None),
            P("section", None, None, None, None, None, None),
            P(),
            P("section", None),
            P("section", None, None),
            P("section", None, None),
        ),
        out_specs=(
            P("section", "shard", None, None),
            P("section", "shard", None, None),
            P("section", None, "shard", None),
        ),
        check_vma=False,
    )
```

time: 2240 us -> 617 us (0.28)
  waiting for transfers between devices: 1540 us -> 360 us
  other arithmetic: 161 us -> 4.53 us
  blocking collectives: 155 us -> 0 us
  local copies, waits for them, and re-layouts: 165 us -> 17.7 us
  matrix products: 131 us -> 3.01 us
  starting transfers between devices: 58.6 us -> 180 us
  Pallas kernels: 0 us -> 23.1 us
    psum x18 -> x0, waiting for transfers between devices: 1490 us -> none  [the longest x9 754 us: run_layer(): updated = (residual + lax.psum(term, 'shard')).astype(jnp.bfloat16)]
    ppermute x11 -> x107, waiting for transfers between devices: 6.25 us -> 335 us  [the longest x105 321 us: send(): return lax.ppermute(value, AXES, pairs_of(move))]
    all_gather x9 -> x0, blocking collectives: 155 us -> none  [run_layer(): fresh_pair = lax.all_gather(fresh_part, 'shard', axis=1, tiled=True)]
    dot_general x90 -> x1, matrix products: 131 us -> 3.01 us  [local(): jnp.einsum('lts,lsd->ltd', pick, pieces, preferred_element_type=f32)]
    ppermute x11 -> x107, starting transfers between devices: 52.1 us -> 174 us  [the longest x105 166 us: send(): return lax.ppermute(value, AXES, pairs_of(move))]
    convert_element_type x38 -> x18, other arithmetic: 51.7 us -> 2.92 us  [the longest x16 2.81 us: local(): summed = sum_parts([term] + [send(term, lambda s, x, z, k=k: (s, x, z + k...]
    scatter x17 -> x0, other arithmetic: 48.5 us -> none
    all_to_all x1, waiting for transfers between devices: 44.8 us -> 0.01 us  [local(): lax.all_to_all(shares, 'section', split_axis=0, concat_axis=0, tiled=True)]
  transfers between devices with their start and end apart: 30 -> 109, of which waited for: 20 -> 71; matrix products, arithmetic and copies ran while one was open for 4% -> 1% of each run, Pallas kernels for 0% -> 1%
where the time goes in v1:
time: 617 us; the launch traced here: 608 us
  waiting for transfers between devices  360 us (58%)
  starting transfers between devices  180 us (29%)
  Pallas kernels  23.1 us (4%)
  between operations  20.2 us (3%)
  local copies, waits for them, and re-layouts  17.7 us (3%)
    ppermute x105, waiting for transfers between devices, send(): return lax.ppermute(value, AXES, pairs_of(move))  321 us
    ppermute x105, starting transfers between devices, send(): return lax.ppermute(value, AXES, pairs_of(move))  166 us
    all_gather x1, waiting for transfers between devices, local(): pair_weight = lax.all_gather(kv_proj[0].T, 'shard', axis=0)  24.7 us
    unnamed x71, local copies, waits for them, and re-layouts  15.7 us
    ppermute x1, waiting for transfers between devices, local(): lax.ppermute(to_right, AXES, [(i, (i + 1) % count) for i in range(count)])  13.7 us
  transfers between devices with their start and end apart: 109, of which 71 were waited for; matrix products, arithmetic and copies ran while one was open for 1% of the time, Pallas kernels for 1%

profile of v1, /device:TPU:1, one launch (start us, length us, event | category | flops | bytes accessed | tf_op | source)
XLA Modules:
  0.0 608.4 jit_solution(18093501892581196674)
XLA Ops:
  14.7 5.0 collective-permute-start.1
  19.8 13.7 %collective-permute-done.left_ref = bf16[8,8,4096]{2,1,0:T(8,128)(2,1)S(1)} collective-permute-done((bf16[8,8,4096]{2,1,0:T(8,128)(2,1)S(1)}, bf16[8,8,4096]{2,1,0:T(8,128)(2,1)S(1)}, u32[]{:S(2)}, u32[]{:S(2)}) %collective-permute-start) | collective-permute-done | bytes 524320 | tf_op jit(solution)/shard_map/ppermute | solution.py:317
  33.4 3.4 build_shares.1
  38.5 5.8 all-to-all-start
  44.5 24.7 %all-gather.3.cloned.1.call-done = bf16[512,4096]{1,0:T(8,128)(2,1)} async-done(((bf16[32,4096]{1,0:T(8,128)(2,1)}), bf16[512,4096]{1,0:T(8,128)(2,1)}) %all-gather.3.cloned.1.call-update) | async-done | bytes 4194320 | tf_op jit(solution)/shard_map/all_gather | solution.py:331
  98.8 5.1 collective-permute-start.10
  104.5 5.5 collective-permute-done.10
  113.3 17.4 %collective-permute-start.11 = (bf16[32,4096]{1,0:T(8,128)(2,1)S(1)}, bf16[32,4096]{1,0:T(8,128)(2,1)S(1)}, u32[]{:S(2)}, u32[]{:S(2)}) collective-permute-start(bf16[32,4096]{1,0:T(8,128)(2,1)S(1)} %add_convert_fusion.14), channel_id=1, source_target_pairs={{0,24},{1,25},{2,26},{3,27},{4,28},{5,29},{6,30},{7,31},{8,16},{9,... | collective-permute-start | bytes 786440 | tf_op jit(solution)/shard_map/ppermute | solution.py:38
  136.1 6.5 %collective-permute-done.12.refs_3_ = bf16[32,4096]{1,0:T(8,128)(2,1)S(1)} collective-permute-done((bf16[32,4096]{1,0:T(8,128)(2,1)S(1)}, bf16[32,4096]{1,0:T(8,128)(2,1)S(1)}, u32[]{:S(2)}, u32[]{:S(2)}) %collective-permute-start.12) | collective-permute-done | bytes 262176 | tf_op jit(solution)/shard_map/ppermute | solution.py:38
  147.4 5.3 attention.9
  156.0 6.4 %collective-permute-done.15 = bf16[32,4096]{1,0:T(8,128)(2,1)S(1)} collective-permute-done((bf16[32,4096]{1,0:T(8,128)(2,1)S(1)}, bf16[32,4096]{1,0:T(8,128)(2,1)S(1)}, u32[]{:S(2)}, u32[]{:S(2)}) %collective-permute-start.15) | collective-permute-done | bytes 262176 | tf_op jit(solution)/shard_map/ppermute | solution.py:38
  162.4 3.5 collective-permute-done.16
  170.6 4.6 collective-permute-done.18.refs_4_
  175.2 6.3 %collective-permute-done.19.refs_5_ = bf16[32,4096]{1,0:T(8,128)(2,1)S(1)} collective-permute-done((bf16[32,4096]{1,0:T(8,128)(2,1)S(1)}, bf16[32,4096]{1,0:T(8,128)(2,1)S(1)}, u32[]{:S(2)}, u32[]{:S(2)}) %collective-permute-start.19) | collective-permute-done | bytes 262176 | tf_op jit(solution)/shard_map/ppermute | solution.py:38
  187.4 6.3 %collective-permute-done.21 = bf16[32,4096]{1,0:T(8,128)(2,1)S(1)} collective-permute-done((bf16[32,4096]{1,0:T(8,128)(2,1)S(1)}, bf16[32,4096]{1,0:T(8,128)(2,1)S(1)}, u32[]{:S(2)}, u32[]{:S(2)}) %collective-permute-start.21) | collective-permute-done | bytes 262176 | tf_op jit(solution)/shard_map/ppermute | solution.py:38
  193.7 4.8 collective-permute-done.22
  203.6 5.6 collective-permute-done.24.refs_2_
  217.2 3.8 collective-permute-done.28
  221.0 8.0 %collective-permute-done.29 = bf16[32,4096]{1,0:T(8,128)(2,1)S(1)} collective-permute-done((bf16[32,4096]{1,0:T(8,128)(2,1)S(1)}, bf16[32,4096]{1,0:T(8,128)(2,1)S(1)}, u32[]{:S(2)}, u32[]{:S(2)}) %collective-permute-start.29) | collective-permute-done | bytes 262176 | tf_op jit(solution)/shard_map/ppermute | solution.py:38
  233.7 4.3 collective-permute-done.31.refs_4_
  238.0 7.0 %collective-permute-done.32.refs_5_ = bf16[32,4096]{1,0:T(8,128)(2,1)S(1)} collective-permute-done((bf16[32,4096]{1,0:T(8,128)(2,1)S(1)}, bf16[32,4096]{1,0:T(8,128)(2,1)S(1)}, u32[]{:S(2)}, u32[]{:S(2)}) %collective-permute-start.32) | collective-permute-done | bytes 262176 | tf_op jit(solution)/shard_map/ppermute | solution.py:38
  248.5 6.2 %collective-permute-done.34 = bf16[32,4096]{1,0:T(8,128)(2,1)S(1)} collective-permute-done((bf16[32,4096]{1,0:T(8,128)(2,1)S(1)}, bf16[32,4096]{1,0:T(8,128)(2,1)S(1)}, u32[]{:S(2)}, u32[]{:S(2)}) %collective-permute-start.34) | collective-permute-done | bytes 262176 | tf_op jit(solution)/shard_map/ppermute | solution.py:38
  254.6 6.0 collective-permute-done.35
  260.9 4.2 collective-permute-start.39
  265.9 5.3 collective-permute-done.37.refs_2_
  271.2 3.3 collective-permute-done.39.refs_4_
  278.4 3.7 collective-permute-done.41
  282.1 6.4 %collective-permute-done.42 = bf16[32,4096]{1,0:T(8,128)(2,1)S(1)} collective-permute-done((bf16[32,4096]{1,0:T(8,128)(2,1)S(1)}, bf16[32,4096]{1,0:T(8,128)(2,1)S(1)}, u32[]{:S(2)}, u32[]{:S(2)}) %collective-permute-start.42) | collective-permute-done | bytes 262176 | tf_op jit(solution)/shard_map/ppermute | solution.py:38
  295.6 7.5 %collective-permute-done.45.refs_5_ = bf16[32,4096]{1,0:T(8,128)(2,1)S(1)} collective-permute-done((bf16[32,4096]{1,0:T(8,128)(2,1)S(1)}, bf16[32,4096]{1,0:T(8,128)(2,1)S(1)}, u32[]{:S(2)}, u32[]{:S(2)}) %collective-permute-start.45) | collective-permute-done | bytes 262176 | tf_op jit(solution)/shard_map/ppermute | solution.py:38
  306.4 5.1 collective-permute-done.47
  311.5 7.1 %collective-permute-done.48 = bf16[32,4096]{1,0:T(8,128)(2,1)S(1)} collective-permute-done((bf16[32,4096]{1,0:T(8,128)(2,1)S(1)}, bf16[32,4096]{1,0:T(8,128)(2,1)S(1)}, u32[]{:S(2)}, u32[]{:S(2)}) %collective-permute-start.48) | collective-permute-done | bytes 262176 | tf_op jit(solution)/shard_map/ppermute | solution.py:38
  318.8 8.3 %collective-permute-start.50 = (bf16[32,4096]{1,0:T(8,128)(2,1)S(1)}, bf16[32,4096]{1,0:T(8,128)(2,1)S(1)}, u32[]{:S(2)}, u32[]{:S(2)}) collective-permute-start(bf16[32,4096]{1,0:T(8,128)(2,1)S(1)} %add_convert_fusion.8), channel_id=1, source_target_pairs={{0,24},{1,25},{2,26},{3,27},{4,28},{5,29},{6,30},{7,31},{8,16},{9,... | collective-permute-start | bytes 786440 | tf_op jit(solution)/shard_map/ppermute | solution.py:38
  332.3 6.8 %collective-permute-done.51.refs_3_ = bf16[32,4096]{1,0:T(8,128)(2,1)S(1)} collective-permute-done((bf16[32,4096]{1,0:T(8,128)(2,1)S(1)}, bf16[32,4096]{1,0:T(8,128)(2,1)S(1)}, u32[]{:S(2)}, u32[]{:S(2)}) %collective-permute-start.51) | collective-permute-done | bytes 262176 | tf_op jit(solution)/shard_map/ppermute | solution.py:38
  342.7 5.3 collective-permute-done.54
  348.0 7.1 %collective-permute-done.55 = bf16[32,4096]{1,0:T(8,128)(2,1)S(1)} collective-permute-done((bf16[32,4096]{1,0:T(8,128)(2,1)S(1)}, bf16[32,4096]{1,0:T(8,128)(2,1)S(1)}, u32[]{:S(2)}, u32[]{:S(2)}) %collective-permute-start.55) | collective-permute-done | bytes 262176 | tf_op jit(solution)/shard_map/ppermute | solution.py:38
  359.4 4.7 collective-permute-done.57.refs_4_
  364.1 6.5 %collective-permute-done.58.refs_5_ = bf16[32,4096]{1,0:T(8,128)(2,1)S(1)} collective-permute-done((bf16[32,4096]{1,0:T(8,128)(2,1)S(1)}, bf16[32,4096]{1,0:T(8,128)(2,1)S(1)}, u32[]{:S(2)}, u32[]{:S(2)}) %collective-permute-start.58) | collective-permute-done | bytes 262176 | tf_op jit(solution)/shard_map/ppermute | solution.py:38
  374.3 5.9 collective-permute-done.60
  380.2 6.4 %collective-permute-done.61 = bf16[32,4096]{1,0:T(8,128)(2,1)S(1)} collective-permute-done((bf16[32,4096]{1,0:T(8,128)(2,1)S(1)}, bf16[32,4096]{1,0:T(8,128)(2,1)S(1)}, u32[]{:S(2)}, u32[]{:S(2)}) %collective-permute-start.61) | collective-permute-done | bytes 262176 | tf_op jit(solution)/shard_map/ppermute | solution.py:38
  391.5 5.1 collective-permute-done.63.refs_2_
  396.6 6.2 %collective-permute-done.65.refs_4_ = bf16[32,4096]{1,0:T(8,128)(2,1)S(1)} collective-permute-done((bf16[32,4096]{1,0:T(8,128)(2,1)S(1)}, bf16[32,4096]{1,0:T(8,128)(2,1)S(1)}, u32[]{:S(2)}, u32[]{:S(2)}) %collective-permute-start.65) | collective-permute-done | bytes 262176 | tf_op jit(solution)/shard_map/ppermute | solution.py:38
  406.6 5.1 collective-permute-done.67
  411.7 7.2 %collective-permute-done.68 = bf16[32,4096]{1,0:T(8,128)(2,1)S(1)} collective-permute-done((bf16[32,4096]{1,0:T(8,128)(2,1)S(1)}, bf16[32,4096]{1,0:T(8,128)(2,1)S(1)}, u32[]{:S(2)}, u32[]{:S(2)}) %collective-permute-start.68) | collective-permute-done | bytes 262176 | tf_op jit(solution)/shard_map/ppermute | solution.py:38
  423.5 4.8 collective-permute-done.70.refs_4_
  428.3 6.4 %collective-permute-done.71.refs_5_ = bf16[32,4096]{1,0:T(8,128)(2,1)S(1)} collective-permute-done((bf16[32,4096]{1,0:T(8,128)(2,1)S(1)}, bf16[32,4096]{1,0:T(8,128)(2,1)S(1)}, u32[]{:S(2)}, u32[]{:S(2)}) %collective-permute-start.71) | collective-permute-done | bytes 262176 | tf_op jit(solution)/shard_map/ppermute | solution.py:38
  438.4 5.9 collective-permute-done.73
  444.3 6.4 %collective-permute-done.74 = bf16[32,4096]{1,0:T(8,128)(2,1)S(1)} collective-permute-done((bf16[32,4096]{1,0:T(8,128)(2,1)S(1)}, bf16[32,4096]{1,0:T(8,128)(2,1)S(1)}, u32[]{:S(2)}, u32[]{:S(2)}) %collective-permute-start.74) | collective-permute-done | bytes 262176 | tf_op jit(solution)/shard_map/ppermute | solution.py:38
  451.5 3.8 collective-permute-start.78
  459.4 5.4 collective-permute-done.78.refs_4_
  468.8 3.6 collective-permute-done.80
  472.4 7.4 %collective-permute-done.81 = bf16[32,4096]{1,0:T(8,128)(2,1)S(1)} collective-permute-done((bf16[32,4096]{1,0:T(8,128)(2,1)S(1)}, bf16[32,4096]{1,0:T(8,128)(2,1)S(1)}, u32[]{:S(2)}, u32[]{:S(2)}) %collective-permute-start.81) | collective-permute-done | bytes 262176 | tf_op jit(solution)/shard_map/ppermute | solution.py:38
  488.1 7.3 %collective-permute-done.84.refs_5_ = bf16[32,4096]{1,0:T(8,128)(2,1)S(1)} collective-permute-done((bf16[32,4096]{1,0:T(8,128)(2,1)S(1)}, bf16[32,4096]{1,0:T(8,128)(2,1)S(1)}, u32[]{:S(2)}, u32[]{:S(2)}) %collective-permute-start.84) | collective-permute-done | bytes 262176 | tf_op jit(solution)/shard_map/ppermute | solution.py:38
  499.4 5.3 collective-permute-done.86
  504.6 6.9 %collective-permute-done.87 = bf16[32,4096]{1,0:T(8,128)(2,1)S(1)} collective-permute-done((bf16[32,4096]{1,0:T(8,128)(2,1)S(1)}, bf16[32,4096]{1,0:T(8,128)(2,1)S(1)}, u32[]{:S(2)}, u32[]{:S(2)}) %collective-permute-start.87) | collective-permute-done | bytes 262176 | tf_op jit(solution)/shard_map/ppermute | solution.py:38
  511.7 4.0 collective-permute-start.89
  522.6 5.1 collective-permute-done.91.refs_4_
  531.6 3.7 collective-permute-done.93
  535.3 8.3 %collective-permute-done.94 = bf16[32,4096]{1,0:T(8,128)(2,1)S(1)} collective-permute-done((bf16[32,4096]{1,0:T(8,128)(2,1)S(1)}, bf16[32,4096]{1,0:T(8,128)(2,1)S(1)}, u32[]{:S(2)}, u32[]{:S(2)}) %collective-permute-start.94) | collective-permute-done | bytes 262176 | tf_op jit(solution)/shard_map/ppermute | solution.py:38
  549.1 3.3 collective-permute-done.96.refs_4_
  552.5 6.7 %collective-permute-done.97.refs_5_ = bf16[32,4096]{1,0:T(8,128)(2,1)S(1)} collective-permute-done((bf16[32,4096]{1,0:T(8,128)(2,1)S(1)}, bf16[32,4096]{1,0:T(8,128)(2,1)S(1)}, u32[]{:S(2)}, u32[]{:S(2)}) %collective-permute-start.97) | collective-permute-done | bytes 262176 | tf_op jit(solution)/shard_map/ppermute | solution.py:38
  562.7 10.6 %collective-permute-done.100 = bf16[32,4096]{1,0:T(8,128)(2,1)S(1)} collective-permute-done((bf16[32,4096]{1,0:T(8,128)(2,1)S(1)}, bf16[32,4096]{1,0:T(8,128)(2,1)S(1)}, u32[]{:S(2)}, u32[]{:S(2)}) %collective-permute-start.100) | collective-permute-done | bytes 262176 | tf_op jit(solution)/shard_map/ppermute | solution.py:38
  574.2 5.7 collective-permute-start.102
  587.5 4.4 collective-permute-done.104
  593.5 3.4 collective-permute-start.106
  (278 shorter events, 187.6 us)
Async XLA Ops:
  7.2 62.1 %all-gather.3.cloned.1.call-start = ((), (), s32[]{:S(2)}) async-start(), calls=%async_computation.1 | async-start | bytes 4456448 | tf_op jit(solution)/shard_map/all_gather | solution.py:331
  12.1 21.3 %collective-permute-start = (bf16[8,8,4096]{2,1,0:T(8,128)(2,1)S(1)}, bf16[8,8,4096]{2,1,0:T(8,128)(2,1)S(1)}, u32[]{:S(2)}, u32[]{:S(2)}) collective-permute-start(bf16[8,8,4096]{2,1,0:T(8,128)(2,1)S(1)} %convolution_convert_fusion), channel_id=1, source_target_pairs={{0,1},{1,2},{2,3},{3,4},{4,5},{5,6},{6,7},{7,8},{8,9},{9,10},{10,1... | collective-permute-start | bytes 1572872 | tf_op jit(solution)/shard_map/ppermute | solution.py:317
  14.7 18.7 %collective-permute-start.1 = (bf16[8,8,4096]{2,1,0:T(8,128)(2,1)S(1)}, bf16[8,8,4096]{2,1,0:T(8,128)(2,1)S(1)}, u32[]{:S(2)}, u32[]{:S(2)}) collective-permute-start(bf16[8,8,4096]{2,1,0:T(8,128)(2,1)S(1)} %slice.36), channel_id=1, source_target_pairs={{1,0},{2,1},{3,2},{4,3},{5,4},{6,5},{7,6},{8,7},{9,8},{10,9},{11,1... | collective-permute-start | bytes 1572872 | tf_op jit(solution)/shard_map/ppermute | solution.py:318
  38.5 53.7 %all-to-all-start = ((bf16[8,48,4096]{2,1,0:T(8,128)(2,1)}), bf16[8,48,4096]{2,1,0:T(8,128)(2,1)S(1)}, u32[]{:S(2)}, u32[]{:S(2)}) async-start(bf16[8,48,4096]{2,1,0:T(8,128)(2,1)} %copy-done.11), calls=%async_computation | async-start | bytes 6291456 | tf_op jit(solution)/shard_map/all_to_all | solution.py:320
  98.8 11.2 %collective-permute-start.10 = (bf16[32,4096]{1,0:T(8,128)(2,1)S(1)}, bf16[32,4096]{1,0:T(8,128)(2,1)S(1)}, u32[]{:S(2)}, u32[]{:S(2)}) collective-permute-start(bf16[32,4096]{1,0:T(8,128)(2,1)S(1)} %experts.8), channel_id=1, source_target_pairs={{0,3},{1,0},{2,1},{3,2},{4,7},{5,4},{6,5},{7,6},{8,11},{9,8},{10,9... | collective-permute-start | bytes 786440 | tf_op jit(solution)/shard_map/ppermute | solution.py:38
  113.3 22.8 %collective-permute-start.11 = (bf16[32,4096]{1,0:T(8,128)(2,1)S(1)}, bf16[32,4096]{1,0:T(8,128)(2,1)S(1)}, u32[]{:S(2)}, u32[]{:S(2)}) collective-permute-start(bf16[32,4096]{1,0:T(8,128)(2,1)S(1)} %add_convert_fusion.14), channel_id=1, source_target_pairs={{0,24},{1,25},{2,26},{3,27},{4,28},{5,29},{6,30},{7,31},{8,16},{9,... | collective-permute-start | bytes 786440 | tf_op jit(solution)/shard_map/ppermute | solution.py:38
  130.6 11.9 %collective-permute-start.12 = (bf16[32,4096]{1,0:T(8,128)(2,1)S(1)}, bf16[32,4096]{1,0:T(8,128)(2,1)S(1)}, u32[]{:S(2)}, u32[]{:S(2)}) collective-permute-start(bf16[32,4096]{1,0:T(8,128)(2,1)S(1)} %add_convert_fusion.14), channel_id=1, source_target_pairs={{0,16},{1,17},{2,18},{3,19},{4,20},{5,21},{6,22},{7,23},{8,24},{9,... | collective-permute-start | bytes 786440 | tf_op jit(solution)/shard_map/ppermute | solution.py:38
  130.8 11.7 %collective-permute-start.13 = (bf16[32,4096]{1,0:T(8,128)(2,1)S(1)}, bf16[32,4096]{1,0:T(8,128)(2,1)S(1)}, u32[]{:S(2)}, u32[]{:S(2)}) collective-permute-start(bf16[32,4096]{1,0:T(8,128)(2,1)S(1)} %add_convert_fusion.14), channel_id=1, source_target_pairs={{0,20},{1,21},{2,22},{3,23},{4,24},{5,25},{6,26},{7,27},{8,28},{9,... | collective-permute-start | bytes 786440 | tf_op jit(solution)/shard_map/ppermute | solution.py:38
  153.4 12.6 %collective-permute-start.16 = (bf16[32,4096]{1,0:T(8,128)(2,1)S(1)}, bf16[32,4096]{1,0:T(8,128)(2,1)S(1)}, u32[]{:S(2)}, u32[]{:S(2)}) collective-permute-start(bf16[32,4096]{1,0:T(8,128)(2,1)S(1)} %get-tuple-element.34), channel_id=1, source_target_pairs={{0,1},{1,2},{2,3},{3,0},{4,5},{5,6},{6,7},{7,4},{8,9},{9,10},{10,1... | collective-permute-start | bytes 786440 | tf_op jit(solution)/shard_map/ppermute | solution.py:38
  153.5 12.4 %collective-permute-start.17 = (bf16[32,4096]{1,0:T(8,128)(2,1)S(1)}, bf16[32,4096]{1,0:T(8,128)(2,1)S(1)}, u32[]{:S(2)}, u32[]{:S(2)}) collective-permute-start(bf16[32,4096]{1,0:T(8,128)(2,1)S(1)} %get-tuple-element.34), channel_id=1, source_target_pairs={{0,3},{1,0},{2,1},{3,2},{4,7},{5,4},{6,5},{7,6},{8,11},{9,8},{10,9... | collective-permute-start | bytes 786440 | tf_op jit(solution)/shard_map/ppermute | solution.py:38
  167.9 13.6 %collective-permute-start.19 = (bf16[32,4096]{1,0:T(8,128)(2,1)S(1)}, bf16[32,4096]{1,0:T(8,128)(2,1)S(1)}, u32[]{:S(2)}, u32[]{:S(2)}) collective-permute-start(bf16[32,4096]{1,0:T(8,128)(2,1)S(1)} %add_convert_fusion.13.refs_3_), channel_id=1, source_target_pairs={{0,4},{1,5},{2,6},{3,7},{4,8},{5,9},{6,10},{7,11},{8,12},{9,13},{1... | collective-permute-start | bytes 786440 | tf_op jit(solution)/shard_map/ppermute | solution.py:38
  168.4 13.1 %collective-permute-start.20 = (bf16[32,4096]{1,0:T(8,128)(2,1)S(1)}, bf16[32,4096]{1,0:T(8,128)(2,1)S(1)}, u32[]{:S(2)}, u32[]{:S(2)}) collective-permute-start(bf16[32,4096]{1,0:T(8,128)(2,1)S(1)} %add_convert_fusion.13.refs_3_), channel_id=1, source_target_pairs={{0,12},{1,13},{2,14},{3,15},{4,0},{5,1},{6,2},{7,3},{8,4},{9,5},{1... | collective-permute-start | bytes 786440 | tf_op jit(solution)/shard_map/ppermute | solution.py:38
  184.7 13.8 %collective-permute-start.22 = (bf16[32,4096]{1,0:T(8,128)(2,1)S(1)}, bf16[32,4096]{1,0:T(8,128)(2,1)S(1)}, u32[]{:S(2)}, u32[]{:S(2)}) collective-permute-start(bf16[32,4096]{1,0:T(8,128)(2,1)S(1)} %experts.9), channel_id=1, source_target_pairs={{0,1},{1,2},{2,3},{3,0},{4,5},{5,6},{6,7},{7,4},{8,9},{9,10},{10,1... | collective-permute-start | bytes 786440 | tf_op jit(solution)/shard_map/ppermute | solution.py:38
  184.9 13.6 %collective-permute-start.23 = (bf16[32,4096]{1,0:T(8,128)(2,1)S(1)}, bf16[32,4096]{1,0:T(8,128)(2,1)S(1)}, u32[]{:S(2)}, u32[]{:S(2)}) collective-permute-start(bf16[32,4096]{1,0:T(8,128)(2,1)S(1)} %experts.9), channel_id=1, source_target_pairs={{0,3},{1,0},{2,1},{3,2},{4,7},{5,4},{6,5},{7,6},{8,11},{9,8},{10,9... | collective-permute-start | bytes 786440 | tf_op jit(solution)/shard_map/ppermute | solution.py:38
  199.7 13.8 %collective-permute-start.26 = (bf16[32,4096]{1,0:T(8,128)(2,1)S(1)}, bf16[32,4096]{1,0:T(8,128)(2,1)S(1)}, u32[]{:S(2)}, u32[]{:S(2)}) collective-permute-start(bf16[32,4096]{1,0:T(8,128)(2,1)S(1)} %add_convert_fusion.12), channel_id=1, source_target_pairs={{0,20},{1,21},{2,22},{3,23},{4,24},{5,25},{6,26},{7,27},{8,28},{9,... | collective-permute-start | bytes 786440 | tf_op jit(solution)/shard_map/ppermute | solution.py:38
  200.6 12.9 %collective-permute-start.27 = (bf16[32,4096]{1,0:T(8,128)(2,1)S(1)}, bf16[32,4096]{1,0:T(8,128)(2,1)S(1)}, u32[]{:S(2)}, u32[]{:S(2)}) collective-permute-start(bf16[32,4096]{1,0:T(8,128)(2,1)S(1)} %add_convert_fusion.12), channel_id=1, source_target_pairs={{0,28},{1,29},{2,30},{3,31},{4,16},{5,17},{6,18},{7,19},{8,20},{9,... | collective-permute-start | bytes 786440 | tf_op jit(solution)/shard_map/ppermute | solution.py:38
  214.6 14.4 %collective-permute-start.29 = (bf16[32,4096]{1,0:T(8,128)(2,1)S(1)}, bf16[32,4096]{1,0:T(8,128)(2,1)S(1)}, u32[]{:S(2)}, u32[]{:S(2)}) collective-permute-start(bf16[32,4096]{1,0:T(8,128)(2,1)S(1)} %get-tuple-element.36), channel_id=1, source_target_pairs={{0,1},{1,2},{2,3},{3,0},{4,5},{5,6},{6,7},{7,4},{8,9},{9,10},{10,1... | collective-permute-start | bytes 786440 | tf_op jit(solution)/shard_map/ppermute | solution.py:38
  215.1 13.9 %collective-permute-start.30 = (bf16[32,4096]{1,0:T(8,128)(2,1)S(1)}, bf16[32,4096]{1,0:T(8,128)(2,1)S(1)}, u32[]{:S(2)}, u32[]{:S(2)}) collective-permute-start(bf16[32,4096]{1,0:T(8,128)(2,1)S(1)} %get-tuple-element.36), channel_id=1, source_target_pairs={{0,3},{1,0},{2,1},{3,2},{4,7},{5,4},{6,5},{7,6},{8,11},{9,8},{10,9... | collective-permute-start | bytes 786440 | tf_op jit(solution)/shard_map/ppermute | solution.py:38
  231.0 14.0 %collective-permute-start.32 = (bf16[32,4096]{1,0:T(8,128)(2,1)S(1)}, bf16[32,4096]{1,0:T(8,128)(2,1)S(1)}, u32[]{:S(2)}, u32[]{:S(2)}) collective-permute-start(bf16[32,4096]{1,0:T(8,128)(2,1)S(1)} %add_convert_fusion.11.refs_3_), channel_id=1, source_target_pairs={{0,4},{1,5},{2,6},{3,7},{4,8},{5,9},{6,10},{7,11},{8,12},{9,13},{1... | collective-permute-start | bytes 786440 | tf_op jit(solution)/shard_map/ppermute | solution.py:38
  231.4 13.6 %collective-permute-start.33 = (bf16[32,4096]{1,0:T(8,128)(2,1)S(1)}, bf16[32,4096]{1,0:T(8,128)(2,1)S(1)}, u32[]{:S(2)}, u32[]{:S(2)}) collective-permute-start(bf16[32,4096]{1,0:T(8,128)(2,1)S(1)} %add_convert_fusion.11.refs_3_), channel_id=1, source_target_pairs={{0,12},{1,13},{2,14},{3,15},{4,0},{5,1},{6,2},{7,3},{8,4},{9,5},{1... | collective-permute-start | bytes 786440 | tf_op jit(solution)/shard_map/ppermute | solution.py:38
  245.7 14.9 %collective-permute-start.35 = (bf16[32,4096]{1,0:T(8,128)(2,1)S(1)}, bf16[32,4096]{1,0:T(8,128)(2,1)S(1)}, u32[]{:S(2)}, u32[]{:S(2)}) collective-permute-start(bf16[32,4096]{1,0:T(8,128)(2,1)S(1)} %experts.10), channel_id=1, source_target_pairs={{0,1},{1,2},{2,3},{3,0},{4,5},{5,6},{6,7},{7,4},{8,9},{9,10},{10,1... | collective-permute-start | bytes 786440 | tf_op jit(solution)/shard_map/ppermute | solution.py:38
  245.8 14.8 %collective-permute-start.36 = (bf16[32,4096]{1,0:T(8,128)(2,1)S(1)}, bf16[32,4096]{1,0:T(8,128)(2,1)S(1)}, u32[]{:S(2)}, u32[]{:S(2)}) collective-permute-start(bf16[32,4096]{1,0:T(8,128)(2,1)S(1)} %experts.10), channel_id=1, source_target_pairs={{0,3},{1,0},{2,1},{3,2},{4,7},{5,4},{6,5},{7,6},{8,11},{9,8},{10,9... | collective-permute-start | bytes 786440 | tf_op jit(solution)/shard_map/ppermute | solution.py:38
  260.9 13.7 %collective-permute-start.39 = (bf16[32,4096]{1,0:T(8,128)(2,1)S(1)}, bf16[32,4096]{1,0:T(8,128)(2,1)S(1)}, u32[]{:S(2)}, u32[]{:S(2)}) collective-permute-start(bf16[32,4096]{1,0:T(8,128)(2,1)S(1)} %add_convert_fusion.10), channel_id=1, source_target_pairs={{0,20},{1,21},{2,22},{3,23},{4,24},{5,25},{6,26},{7,27},{8,28},{9,... | collective-permute-start | bytes 786440 | tf_op jit(solution)/shard_map/ppermute | solution.py:38
  275.7 12.8 %collective-permute-start.42 = (bf16[32,4096]{1,0:T(8,128)(2,1)S(1)}, bf16[32,4096]{1,0:T(8,128)(2,1)S(1)}, u32[]{:S(2)}, u32[]{:S(2)}) collective-permute-start(bf16[32,4096]{1,0:T(8,128)(2,1)S(1)} %get-tuple-element.38), channel_id=1, source_target_pairs={{0,1},{1,2},{2,3},{3,0},{4,5},{5,6},{6,7},{7,4},{8,9},{9,10},{10,1... | collective-permute-start | bytes 786440 | tf_op jit(solution)/shard_map/ppermute | solution.py:38
  275.8 12.8 %collective-permute-start.43 = (bf16[32,4096]{1,0:T(8,128)(2,1)S(1)}, bf16[32,4096]{1,0:T(8,128)(2,1)S(1)}, u32[]{:S(2)}, u32[]{:S(2)}) collective-permute-start(bf16[32,4096]{1,0:T(8,128)(2,1)S(1)} %get-tuple-element.38), channel_id=1, source_target_pairs={{0,3},{1,0},{2,1},{3,2},{4,7},{5,4},{6,5},{7,6},{8,11},{9,8},{10,9... | collective-permute-start | bytes 786440 | tf_op jit(solution)/shard_map/ppermute | solution.py:38
  290.6 12.4 %collective-permute-start.45 = (bf16[32,4096]{1,0:T(8,128)(2,1)S(1)}, bf16[32,4096]{1,0:T(8,128)(2,1)S(1)}, u32[]{:S(2)}, u32[]{:S(2)}) collective-permute-start(bf16[32,4096]{1,0:T(8,128)(2,1)S(1)} %add_convert_fusion.9.refs_3_), channel_id=1, source_target_pairs={{0,4},{1,5},{2,6},{3,7},{4,8},{5,9},{6,10},{7,11},{8,12},{9,13},{1... | collective-permute-start | bytes 786440 | tf_op jit(solution)/shard_map/ppermute | solution.py:38
  290.7 12.4 %collective-permute-start.46 = (bf16[32,4096]{1,0:T(8,128)(2,1)S(1)}, bf16[32,4096]{1,0:T(8,128)(2,1)S(1)}, u32[]{:S(2)}, u32[]{:S(2)}) collective-permute-start(bf16[32,4096]{1,0:T(8,128)(2,1)S(1)} %add_convert_fusion.9.refs_3_), channel_id=1, source_target_pairs={{0,12},{1,13},{2,14},{3,15},{4,0},{5,1},{6,2},{7,3},{8,4},{9,5},{1... | collective-permute-start | bytes 786440 | tf_op jit(solution)/shard_map/ppermute | solution.py:38
  303.7 14.9 %collective-permute-start.48 = (bf16[32,4096]{1,0:T(8,128)(2,1)S(1)}, bf16[32,4096]{1,0:T(8,128)(2,1)S(1)}, u32[]{:S(2)}, u32[]{:S(2)}) collective-permute-start(bf16[32,4096]{1,0:T(8,128)(2,1)S(1)} %experts.11), channel_id=1, source_target_pairs={{0,1},{1,2},{2,3},{3,0},{4,5},{5,6},{6,7},{7,4},{8,9},{9,10},{10,1... | collective-permute-start | bytes 786440 | tf_op jit(solution)/shard_map/ppermute | solution.py:38
  303.8 14.8 %collective-permute-start.49 = (bf16[32,4096]{1,0:T(8,128)(2,1)S(1)}, bf16[32,4096]{1,0:T(8,128)(2,1)S(1)}, u32[]{:S(2)}, u32[]{:S(2)}) collective-permute-start(bf16[32,4096]{1,0:T(8,128)(2,1)S(1)} %experts.11), channel_id=1, source_target_pairs={{0,3},{1,0},{2,1},{3,2},{4,7},{5,4},{6,5},{7,6},{8,11},{9,8},{10,9... | collective-permute-start | bytes 786440 | tf_op jit(solution)/shard_map/ppermute | solution.py:38
  318.8 13.5 %collective-permute-start.50 = (bf16[32,4096]{1,0:T(8,128)(2,1)S(1)}, bf16[32,4096]{1,0:T(8,128)(2,1)S(1)}, u32[]{:S(2)}, u32[]{:S(2)}) collective-permute-start(bf16[32,4096]{1,0:T(8,128)(2,1)S(1)} %add_convert_fusion.8), channel_id=1, source_target_pairs={{0,24},{1,25},{2,26},{3,27},{4,28},{5,29},{6,30},{7,31},{8,16},{9,... | collective-permute-start | bytes 786440 | tf_op jit(solution)/shard_map/ppermute | solution.py:38
  327.0 12.0 %collective-permute-start.51 = (bf16[32,4096]{1,0:T(8,128)(2,1)S(1)}, bf16[32,4096]{1,0:T(8,128)(2,1)S(1)}, u32[]{:S(2)}, u32[]{:S(2)}) collective-permute-start(bf16[32,4096]{1,0:T(8,128)(2,1)S(1)} %add_convert_fusion.8), channel_id=1, source_target_pairs={{0,16},{1,17},{2,18},{3,19},{4,20},{5,21},{6,22},{7,23},{8,24},{9,... | collective-permute-start | bytes 786440 | tf_op jit(solution)/shard_map/ppermute | solution.py:38
  327.3 11.7 %collective-permute-start.52 = (bf16[32,4096]{1,0:T(8,128)(2,1)S(1)}, bf16[32,4096]{1,0:T(8,128)(2,1)S(1)}, u32[]{:S(2)}, u32[]{:S(2)}) collective-permute-start(bf16[32,4096]{1,0:T(8,128)(2,1)S(1)} %add_convert_fusion.8), channel_id=1, source_target_pairs={{0,20},{1,21},{2,22},{3,23},{4,24},{5,25},{6,26},{7,27},{8,28},{9,... | collective-permute-start | bytes 786440 | tf_op jit(solution)/shard_map/ppermute | solution.py:38
  328.2 10.9 %collective-permute-start.53 = (bf16[32,4096]{1,0:T(8,128)(2,1)S(1)}, bf16[32,4096]{1,0:T(8,128)(2,1)S(1)}, u32[]{:S(2)}, u32[]{:S(2)}) collective-permute-start(bf16[32,4096]{1,0:T(8,128)(2,1)S(1)} %add_convert_fusion.8), channel_id=1, source_target_pairs={{0,28},{1,29},{2,30},{3,31},{4,16},{5,17},{6,18},{7,19},{8,20},{9,... | collective-permute-start | bytes 786440 | tf_op jit(solution)/shard_map/ppermute | solution.py:38
  340.0 15.0 %collective-permute-start.55 = (bf16[32,4096]{1,0:T(8,128)(2,1)S(1)}, bf16[32,4096]{1,0:T(8,128)(2,1)S(1)}, u32[]{:S(2)}, u32[]{:S(2)}) collective-permute-start(bf16[32,4096]{1,0:T(8,128)(2,1)S(1)} %get-tuple-element.40), channel_id=1, source_target_pairs={{0,1},{1,2},{2,3},{3,0},{4,5},{5,6},{6,7},{7,4},{8,9},{9,10},{10,1... | collective-permute-start | bytes 786440 | tf_op jit(solution)/shard_map/ppermute | solution.py:38
  340.5 14.5 %collective-permute-start.56 = (bf16[32,4096]{1,0:T(8,128)(2,1)S(1)}, bf16[32,4096]{1,0:T(8,128)(2,1)S(1)}, u32[]{:S(2)}, u32[]{:S(2)}) collective-permute-start(bf16[32,4096]{1,0:T(8,128)(2,1)S(1)} %get-tuple-element.40), channel_id=1, source_target_pairs={{0,3},{1,0},{2,1},{3,2},{4,7},{5,4},{6,5},{7,6},{8,11},{9,8},{10,9... | collective-permute-start | bytes 786440 | tf_op jit(solution)/shard_map/ppermute | solution.py:38
  356.8 13.9 %collective-permute-start.58 = (bf16[32,4096]{1,0:T(8,128)(2,1)S(1)}, bf16[32,4096]{1,0:T(8,128)(2,1)S(1)}, u32[]{:S(2)}, u32[]{:S(2)}) collective-permute-start(bf16[32,4096]{1,0:T(8,128)(2,1)S(1)} %add_convert_fusion.7.refs_3_), channel_id=1, source_target_pairs={{0,4},{1,5},{2,6},{3,7},{4,8},{5,9},{6,10},{7,11},{8,12},{9,13},{1... | collective-permute-start | bytes 786440 | tf_op jit(solution)/shard_map/ppermute | solution.py:38
  357.0 13.6 %collective-permute-start.59 = (bf16[32,4096]{1,0:T(8,128)(2,1)S(1)}, bf16[32,4096]{1,0:T(8,128)(2,1)S(1)}, u32[]{:S(2)}, u32[]{:S(2)}) collective-permute-start(bf16[32,4096]{1,0:T(8,128)(2,1)S(1)} %add_convert_fusion.7.refs_3_), channel_id=1, source_target_pairs={{0,12},{1,13},{2,14},{3,15},{4,0},{5,1},{6,2},{7,3},{8,4},{9,5},{1... | collective-permute-start | bytes 786440 | tf_op jit(solution)/shard_map/ppermute | solution.py:38
  371.6 15.0 %collective-permute-start.61 = (bf16[32,4096]{1,0:T(8,128)(2,1)S(1)}, bf16[32,4096]{1,0:T(8,128)(2,1)S(1)}, u32[]{:S(2)}, u32[]{:S(2)}) collective-permute-start(bf16[32,4096]{1,0:T(8,128)(2,1)S(1)} %experts.12), channel_id=1, source_target_pairs={{0,1},{1,2},{2,3},{3,0},{4,5},{5,6},{6,7},{7,4},{8,9},{9,10},{10,1... | collective-permute-start | bytes 786440 | tf_op jit(solution)/shard_map/ppermute | solution.py:38
  371.6 15.0 %collective-permute-start.62 = (bf16[32,4096]{1,0:T(8,128)(2,1)S(1)}, bf16[32,4096]{1,0:T(8,128)(2,1)S(1)}, u32[]{:S(2)}, u32[]{:S(2)}) collective-permute-start(bf16[32,4096]{1,0:T(8,128)(2,1)S(1)} %experts.12), channel_id=1, source_target_pairs={{0,3},{1,0},{2,1},{3,2},{4,7},{5,4},{6,5},{7,6},{8,11},{9,8},{10,9... | collective-permute-start | bytes 786440 | tf_op jit(solution)/shard_map/ppermute | solution.py:38
  389.4 13.5 %collective-permute-start.65 = (bf16[32,4096]{1,0:T(8,128)(2,1)S(1)}, bf16[32,4096]{1,0:T(8,128)(2,1)S(1)}, u32[]{:S(2)}, u32[]{:S(2)}) collective-permute-start(bf16[32,4096]{1,0:T(8,128)(2,1)S(1)} %add_convert_fusion.6), channel_id=1, source_target_pairs={{0,20},{1,21},{2,22},{3,23},{4,24},{5,25},{6,26},{7,27},{8,28},{9,... | collective-permute-start | bytes 786440 | tf_op jit(solution)/shard_map/ppermute | solution.py:38
  390.6 12.2 %collective-permute-start.66 = (bf16[32,4096]{1,0:T(8,128)(2,1)S(1)}, bf16[32,4096]{1,0:T(8,128)(2,1)S(1)}, u32[]{:S(2)}, u32[]{:S(2)}) collective-permute-start(bf16[32,4096]{1,0:T(8,128)(2,1)S(1)} %add_convert_fusion.6), channel_id=1, source_target_pairs={{0,28},{1,29},{2,30},{3,31},{4,16},{5,17},{6,18},{7,19},{8,20},{9,... | collective-permute-start | bytes 786440 | tf_op jit(solution)/shard_map/ppermute | solution.py:38
  403.9 15.0 %collective-permute-start.68 = (bf16[32,4096]{1,0:T(8,128)(2,1)S(1)}, bf16[32,4096]{1,0:T(8,128)(2,1)S(1)}, u32[]{:S(2)}, u32[]{:S(2)}) collective-permute-start(bf16[32,4096]{1,0:T(8,128)(2,1)S(1)} %get-tuple-element.42), channel_id=1, source_target_pairs={{0,1},{1,2},{2,3},{3,0},{4,5},{5,6},{6,7},{7,4},{8,9},{9,10},{10,1... | collective-permute-start | bytes 786440 | tf_op jit(solution)/shard_map/ppermute | solution.py:38
  403.9 15.0 %collective-permute-start.69 = (bf16[32,4096]{1,0:T(8,128)(2,1)S(1)}, bf16[32,4096]{1,0:T(8,128)(2,1)S(1)}, u32[]{:S(2)}, u32[]{:S(2)}) collective-permute-start(bf16[32,4096]{1,0:T(8,128)(2,1)S(1)} %get-tuple-element.42), channel_id=1, source_target_pairs={{0,3},{1,0},{2,1},{3,2},{4,7},{5,4},{6,5},{7,6},{8,11},{9,8},{10,9... | collective-permute-start | bytes 786440 | tf_op jit(solution)/shard_map/ppermute | solution.py:38
  420.8 13.9 %collective-permute-start.71 = (bf16[32,4096]{1,0:T(8,128)(2,1)S(1)}, bf16[32,4096]{1,0:T(8,128)(2,1)S(1)}, u32[]{:S(2)}, u32[]{:S(2)}) collective-permute-start(bf16[32,4096]{1,0:T(8,128)(2,1)S(1)} %add_convert_fusion.5.refs_3_), channel_id=1, source_target_pairs={{0,4},{1,5},{2,6},{3,7},{4,8},{5,9},{6,10},{7,11},{8,12},{9,13},{1... | collective-permute-start | bytes 786440 | tf_op jit(solution)/shard_map/ppermute | solution.py:38
  420.8 13.9 %collective-permute-start.72 = (bf16[32,4096]{1,0:T(8,128)(2,1)S(1)}, bf16[32,4096]{1,0:T(8,128)(2,1)S(1)}, u32[]{:S(2)}, u32[]{:S(2)}) collective-permute-start(bf16[32,4096]{1,0:T(8,128)(2,1)S(1)} %add_convert_fusion.5.refs_3_), channel_id=1, source_target_pairs={{0,12},{1,13},{2,14},{3,15},{4,0},{5,1},{6,2},{7,3},{8,4},{9,5},{1... | collective-permute-start | bytes 786440 | tf_op jit(solution)/shard_map/ppermute | solution.py:38
  435.7 15.0 %collective-permute-start.74 = (bf16[32,4096]{1,0:T(8,128)(2,1)S(1)}, bf16[32,4096]{1,0:T(8,128)(2,1)S(1)}, u32[]{:S(2)}, u32[]{:S(2)}) collective-permute-start(bf16[32,4096]{1,0:T(8,128)(2,1)S(1)} %experts.13), channel_id=1, source_target_pairs={{0,1},{1,2},{2,3},{3,0},{4,5},{5,6},{6,7},{7,4},{8,9},{9,10},{10,1... | collective-permute-start | bytes 786440 | tf_op jit(solution)/shard_map/ppermute | solution.py:38
  435.7 15.0 %collective-permute-start.75 = (bf16[32,4096]{1,0:T(8,128)(2,1)S(1)}, bf16[32,4096]{1,0:T(8,128)(2,1)S(1)}, u32[]{:S(2)}, u32[]{:S(2)}) collective-permute-start(bf16[32,4096]{1,0:T(8,128)(2,1)S(1)} %experts.13), channel_id=1, source_target_pairs={{0,3},{1,0},{2,1},{3,2},{4,7},{5,4},{6,5},{7,6},{8,11},{9,8},{10,9... | collective-permute-start | bytes 786440 | tf_op jit(solution)/shard_map/ppermute | solution.py:38
  451.5 13.3 %collective-permute-start.78 = (bf16[32,4096]{1,0:T(8,128)(2,1)S(1)}, bf16[32,4096]{1,0:T(8,128)(2,1)S(1)}, u32[]{:S(2)}, u32[]{:S(2)}) collective-permute-start(bf16[32,4096]{1,0:T(8,128)(2,1)S(1)} %add_convert_fusion.4), channel_id=1, source_target_pairs={{0,20},{1,21},{2,22},{3,23},{4,24},{5,25},{6,26},{7,27},{8,28},{9,... | collective-permute-start | bytes 786440 | tf_op jit(solution)/shard_map/ppermute | solution.py:38
  466.2 13.6 %collective-permute-start.81 = (bf16[32,4096]{1,0:T(8,128)(2,1)S(1)}, bf16[32,4096]{1,0:T(8,128)(2,1)S(1)}, u32[]{:S(2)}, u32[]{:S(2)}) collective-permute-start(bf16[32,4096]{1,0:T(8,128)(2,1)S(1)} %get-tuple-element.44), channel_id=1, source_target_pairs={{0,1},{1,2},{2,3},{3,0},{4,5},{5,6},{6,7},{7,4},{8,9},{9,10},{10,1... | collective-permute-start | bytes 786440 | tf_op jit(solution)/shard_map/ppermute | solution.py:38
  466.2 13.6 %collective-permute-start.82 = (bf16[32,4096]{1,0:T(8,128)(2,1)S(1)}, bf16[32,4096]{1,0:T(8,128)(2,1)S(1)}, u32[]{:S(2)}, u32[]{:S(2)}) collective-permute-start(bf16[32,4096]{1,0:T(8,128)(2,1)S(1)} %get-tuple-element.44), channel_id=1, source_target_pairs={{0,3},{1,0},{2,1},{3,2},{4,7},{5,4},{6,5},{7,6},{8,11},{9,8},{10,9... | collective-permute-start | bytes 786440 | tf_op jit(solution)/shard_map/ppermute | solution.py:38
  483.2 12.2 %collective-permute-start.84 = (bf16[32,4096]{1,0:T(8,128)(2,1)S(1)}, bf16[32,4096]{1,0:T(8,128)(2,1)S(1)}, u32[]{:S(2)}, u32[]{:S(2)}) collective-permute-start(bf16[32,4096]{1,0:T(8,128)(2,1)S(1)} %add_convert_fusion.3.refs_3_), channel_id=1, source_target_pairs={{0,4},{1,5},{2,6},{3,7},{4,8},{5,9},{6,10},{7,11},{8,12},{9,13},{1... | collective-permute-start | bytes 786440 | tf_op jit(solution)/shard_map/ppermute | solution.py:38
  484.4 11.6 %collective-permute-start.85 = (bf16[32,4096]{1,0:T(8,128)(2,1)S(1)}, bf16[32,4096]{1,0:T(8,128)(2,1)S(1)}, u32[]{:S(2)}, u32[]{:S(2)}) collective-permute-start(bf16[32,4096]{1,0:T(8,128)(2,1)S(1)} %add_convert_fusion.3.refs_3_), channel_id=1, source_target_pairs={{0,12},{1,13},{2,14},{3,15},{4,0},{5,1},{6,2},{7,3},{8,4},{9,5},{1... | collective-permute-start | bytes 786440 | tf_op jit(solution)/shard_map/ppermute | solution.py:38
  496.6 14.9 %collective-permute-start.87 = (bf16[32,4096]{1,0:T(8,128)(2,1)S(1)}, bf16[32,4096]{1,0:T(8,128)(2,1)S(1)}, u32[]{:S(2)}, u32[]{:S(2)}) collective-permute-start(bf16[32,4096]{1,0:T(8,128)(2,1)S(1)} %experts.14), channel_id=1, source_target_pairs={{0,1},{1,2},{2,3},{3,0},{4,5},{5,6},{6,7},{7,4},{8,9},{9,10},{10,1... | collective-permute-start | bytes 786440 | tf_op jit(solution)/shard_map/ppermute | solution.py:38
  496.7 14.8 %collective-permute-start.88 = (bf16[32,4096]{1,0:T(8,128)(2,1)S(1)}, bf16[32,4096]{1,0:T(8,128)(2,1)S(1)}, u32[]{:S(2)}, u32[]{:S(2)}) collective-permute-start(bf16[32,4096]{1,0:T(8,128)(2,1)S(1)} %experts.14), channel_id=1, source_target_pairs={{0,3},{1,0},{2,1},{3,2},{4,7},{5,4},{6,5},{7,6},{8,11},{9,8},{10,9... | collective-permute-start | bytes 786440 | tf_op jit(solution)/shard_map/ppermute | solution.py:38
  515.8 11.9 %collective-permute-start.91 = (bf16[32,4096]{1,0:T(8,128)(2,1)S(1)}, bf16[32,4096]{1,0:T(8,128)(2,1)S(1)}, u32[]{:S(2)}, u32[]{:S(2)}) collective-permute-start(bf16[32,4096]{1,0:T(8,128)(2,1)S(1)} %add_convert_fusion.2), channel_id=1, source_target_pairs={{0,20},{1,21},{2,22},{3,23},{4,24},{5,25},{6,26},{7,27},{8,28},{9,... | collective-permute-start | bytes 786440 | tf_op jit(solution)/shard_map/ppermute | solution.py:38
  528.9 14.7 %collective-permute-start.94 = (bf16[32,4096]{1,0:T(8,128)(2,1)S(1)}, bf16[32,4096]{1,0:T(8,128)(2,1)S(1)}, u32[]{:S(2)}, u32[]{:S(2)}) collective-permute-start(bf16[32,4096]{1,0:T(8,128)(2,1)S(1)} %get-tuple-element.46), channel_id=1, source_target_pairs={{0,1},{1,2},{2,3},{3,0},{4,5},{5,6},{6,7},{7,4},{8,9},{9,10},{10,1... | collective-permute-start | bytes 786440 | tf_op jit(solution)/shard_map/ppermute | solution.py:38
  529.5 14.1 %collective-permute-start.95 = (bf16[32,4096]{1,0:T(8,128)(2,1)S(1)}, bf16[32,4096]{1,0:T(8,128)(2,1)S(1)}, u32[]{:S(2)}, u32[]{:S(2)}) collective-permute-start(bf16[32,4096]{1,0:T(8,128)(2,1)S(1)} %get-tuple-element.46), channel_id=1, source_target_pairs={{0,3},{1,0},{2,1},{3,2},{4,7},{5,4},{6,5},{7,6},{8,11},{9,8},{10,9... | collective-permute-start | bytes 786440 | tf_op jit(solution)/shard_map/ppermute | solution.py:38
  546.5 12.7 %collective-permute-start.97 = (bf16[32,4096]{1,0:T(8,128)(2,1)S(1)}, bf16[32,4096]{1,0:T(8,128)(2,1)S(1)}, u32[]{:S(2)}, u32[]{:S(2)}) collective-permute-start(bf16[32,4096]{1,0:T(8,128)(2,1)S(1)} %add_convert_fusion.1.refs_3_), channel_id=1, source_target_pairs={{0,4},{1,5},{2,6},{3,7},{4,8},{5,9},{6,10},{7,11},{8,12},{9,13},{1... | collective-permute-start | bytes 786440 | tf_op jit(solution)/shard_map/ppermute | solution.py:38
  547.8 11.6 %collective-permute-start.98 = (bf16[32,4096]{1,0:T(8,128)(2,1)S(1)}, bf16[32,4096]{1,0:T(8,128)(2,1)S(1)}, u32[]{:S(2)}, u32[]{:S(2)}) collective-permute-start(bf16[32,4096]{1,0:T(8,128)(2,1)S(1)} %add_convert_fusion.1.refs_3_), channel_id=1, source_target_pairs={{0,12},{1,13},{2,14},{3,15},{4,0},{5,1},{6,2},{7,3},{8,4},{9,5},{1... | collective-permute-start | bytes 786440 | tf_op jit(solution)/shard_map/ppermute | solution.py:38
  560.0 13.4 %collective-permute-start.100 = (bf16[32,4096]{1,0:T(8,128)(2,1)S(1)}, bf16[32,4096]{1,0:T(8,128)(2,1)S(1)}, u32[]{:S(2)}, u32[]{:S(2)}) collective-permute-start(bf16[32,4096]{1,0:T(8,128)(2,1)S(1)} %experts.15), channel_id=1, source_target_pairs={{0,1},{1,2},{2,3},{3,0},{4,5},{5,6},{6,7},{7,4},{8,9},{9,10},{10,1... | collective-permute-start | bytes 786440 | tf_op jit(solution)/shard_map/ppermute | solution.py:38
  560.1 13.3 %collective-permute-start.101 = (bf16[32,4096]{1,0:T(8,128)(2,1)S(1)}, bf16[32,4096]{1,0:T(8,128)(2,1)S(1)}, u32[]{:S(2)}, u32[]{:S(2)}) collective-permute-start(bf16[32,4096]{1,0:T(8,128)(2,1)S(1)} %experts.15), channel_id=1, source_target_pairs={{0,3},{1,0},{2,1},{3,2},{4,7},{5,4},{6,5},{7,6},{8,11},{9,8},{10,9... | collective-permute-start | bytes 786440 | tf_op jit(solution)/shard_map/ppermute | solution.py:38
  574.2 13.3 %collective-permute-start.102 = (bf16[32,4096]{1,0:T(8,128)(2,1)}, bf16[32,4096]{1,0:T(8,128)(2,1)}, u32[]{:S(2)}, u32[]{:S(2)}) collective-permute-start(bf16[32,4096]{1,0:T(8,128)(2,1)} %add_convert_fusion), channel_id=1, source_target_pairs={{0,24},{1,25},{2,26},{3,27},{4,28},{5,29},{6,30},{7,31},{8,16},{9,... | collective-permute-start | bytes 786440 | tf_op jit(solution)/shard_map/ppermute | solution.py:38
  579.9 12.0 %collective-permute-start.104 = (bf16[32,4096]{1,0:T(8,128)(2,1)}, bf16[32,4096]{1,0:T(8,128)(2,1)}, u32[]{:S(2)}, u32[]{:S(2)}) collective-permute-start(bf16[32,4096]{1,0:T(8,128)(2,1)} %add_convert_fusion), channel_id=1, source_target_pairs={{0,20},{1,21},{2,22},{3,23},{4,24},{5,25},{6,26},{7,27},{8,28},{9,... | collective-permute-start | bytes 786440 | tf_op jit(solution)/shard_map/ppermute | solution.py:38
  580.8 11.1 %collective-permute-start.105 = (bf16[32,4096]{1,0:T(8,128)(2,1)}, bf16[32,4096]{1,0:T(8,128)(2,1)}, u32[]{:S(2)}, u32[]{:S(2)}) collective-permute-start(bf16[32,4096]{1,0:T(8,128)(2,1)} %add_convert_fusion), channel_id=1, source_target_pairs={{0,28},{1,29},{2,30},{3,31},{4,16},{5,17},{6,18},{7,19},{8,20},{9,... | collective-permute-start | bytes 786440 | tf_op jit(solution)/shard_map/ppermute | solution.py:38
  (79 other events, 1223.6 us)
Sparse Core Ops, SparseCore 0:
  10.1 59.0 all-gather.2
